TPU v7x, 768 devices: a whole 4x8x12 slice. The times are simulated.
768 devices in a mesh: row: 16 (over x, z_lo), col: 8 (over y), rep: 6 (over z_hi, core).
Axes of the slice: x: 4, y: 8, z: 12 (z_hi: 3, z_lo: 4; z = z_hi * 4 + z_lo), core: 2. Of those that a mesh axis runs over, the one named last changes fastest.
Arguments:
- features: bfloat16 [16, 6144, 256], P('row', ('col', 'rep')), may hold values from -6 to 6
- adj_tiles: bfloat16 [16, 48, 32, 128, 128], P('row', ('col', 'rep'))
- tile_rows: int32 [16, 48, 32], P('row', ('col', 'rep')), may hold values from 0 to 47
- tile_cols: int32 [16, 48, 32], P('row', ('col', 'rep')), may hold values from 0 to 15
- tile_count: int32 [16, 48], P('row', ('col', 'rep')), may hold values from 4 to 32, as said below
- weight: bfloat16 [256, 256], replicated, may hold values from -0.375 to 0.375
- cotangent: bfloat16 [98304, 256], P('row'), may hold values from -6 to 6
Outputs:
- layer_out: bfloat16 [98304, 256], P(('row', 'col', 'rep'))
- feature_grad: bfloat16 [16, 6144, 256], P('row', ('col', 'rep'))
Inputs may be any that keep to these rules, and one draw needn't show every extreme that they name: `tile_count`: slots at or past a grid cell's count are not part of the adjacency. Each count is 32 divided by 1, 2, 4 or 8, and some grid cell holds 32.
All inputs are finite; a program needn't handle non-finite values.
Results may differ from a plain program's by a relative error of at most 0.025.
Values may be sent and summed in bfloat16 or wider, within the bound.
No kernel may reach another device: no remote copies, remote signals or barrier semaphores. Data moves between devices by JAX's collectives and lax.ppermute only.
A program may use at most 64 MiB of HBM per device.

v0:
```python
import jax
import jax.numpy as jnp
from jax import lax
from jax.sharding import PartitionSpec as P


def tile_sum(adj_slabs, src_index, out_index, live_count, source, out_tiles, einsum_form):
    picked = jnp.take(source, src_index, axis=0)
    product = jnp.einsum(einsum_form, adj_slabs, picked, preferred_element_type=jnp.float32)
    slot = jnp.arange(adj_slabs.shape[0], dtype=jnp.int32)
    live_mask = slot < live_count
    target = jnp.arange(out_tiles, dtype=jnp.int32)
    onehot = ((out_index[None, :] == target[:, None]) & live_mask[None, :]).astype(jnp.bfloat16)
    upper = product.astype(jnp.bfloat16)
    lower = (product - upper.astype(jnp.float32)).astype(jnp.bfloat16)
    summed = jnp.einsum("rt,tif->rif", onehot, upper, preferred_element_type=jnp.float32)
    summed = summed + jnp.einsum("rt,tif->rif", onehot, lower, preferred_element_type=jnp.float32)
    return summed.reshape(out_tiles * adj_slabs.shape[1], -1)


def pre_grad(pre_act, own_grad):
    sigma = jax.nn.sigmoid(pre_act)
    return (own_grad.astype(jnp.float32) * sigma * (1.0 + pre_act * (1.0 - sigma))).astype(
        jnp.bfloat16
    )


def back_project(grad_low, weight):
    return jnp.einsum("nf,gf->ng", grad_low, weight, preferred_element_type=jnp.float32).astype(
        jnp.bfloat16
    )


def per_device(features, adj_tiles, tile_rows, tile_cols, tile_count, weight, cotangent):
    feat_width = weight.shape[1]
    tile_len = adj_tiles.shape[-1]
    section_count = lax.axis_size(("col", "rep"))
    row_len = cotangent.shape[0]
    node_dev = row_len // section_count
    panels = lax.all_gather(features, "row", axis=0, tiled=True)
    col_len = panels.shape[0] * panels.shape[1]
    adj_slabs = adj_tiles[0, 0]
    slab_rows = tile_rows[0, 0]
    slab_cols = tile_cols[0, 0]
    live_count = tile_count[0, 0]
    partial_value = tile_sum(
        adj_slabs, slab_cols, slab_rows, live_count, panels, row_len // tile_len, "tij,tjf->tif"
    )
    offset = lax.axis_index(("col", "rep")) * node_dev
    sum_piece = lax.psum_scatter(partial_value, ("col", "rep"), scatter_dimension=0, tiled=True)
    pre_act = jnp.dot(sum_piece.astype(jnp.bfloat16), weight, preferred_element_type=jnp.float32)
    layer_out = jax.nn.silu(pre_act).astype(jnp.bfloat16)
    own_grad = lax.dynamic_slice_in_dim(cotangent, offset, node_dev, 0)
    grad_piece = back_project(pre_grad(pre_act, own_grad), weight)
    grad_rows = lax.all_gather(grad_piece, ("col", "rep"), axis=0, tiled=True)
    grad_source = grad_rows.reshape(row_len // tile_len, tile_len, feat_width)
    column_part = tile_sum(
        adj_slabs,
        slab_rows,
        slab_cols,
        live_count,
        grad_source,
        col_len // tile_len,
        "tji,tjf->tif",
    )
    grad_input = lax.psum_scatter(
        column_part.astype(jnp.bfloat16), "row", scatter_dimension=0, tiled=True
    )
    return (layer_out, grad_input[None])


def solution(mesh):
    in_specs = (
        P("row", ("col", "rep"), None),
        P("row", ("col", "rep"), None, None, None),
        P("row", ("col", "rep"), None),
        P("row", ("col", "rep"), None),
        P("row", ("col", "rep")),
        P(),
        P("row", None),
    )
    out_specs = (P(("row", "col", "rep"), None), P("row", ("col", "rep"), None))
    return jax.shard_map(
        per_device, mesh=mesh, in_specs=in_specs, out_specs=out_specs, check_vma=False
    )
```

profile of v0, /device:TPU:24, one launch (start us, length us, event | category | flops | bytes accessed | tf_op | source)
XLA Modules:
  0.0 579.1 jit_solution(18170117759241948925)
XLA Ops:
  7.2 0.7 all-gather.3.cloned.1.call-update
  8.6 0.7 fusion.34
  9.3 0.7 compare_and_fusion.1
  9.9 94.8 %all-gather.3.cloned.1.call-done = bf16[16,128,256]{2,1,0:T(8,128)(2,1)} async-done(((bf16[1,128,256]{2,1,0:T(8,128)(2,1)}), bf16[16,128,256]{2,1,0:T(8,128)(2,1)}) %all-gather.3.cloned.1.call-update) | async-done | bytes 1048592 | tf_op jit(solution)/shard_map/all_gather | solution.py:40
  104.7 1.9 gather_fusion
  106.6 3.0 fusion.1
  109.7 3.4 copy.24
  113.1 4.6 copy.25
  117.6 1.1 fusion.19
  118.7 0.5 copy-done.2
  119.2 1.1 convolution_add_fusion
  120.3 6.3 %copy.26 = f32[48,128,256]{2,1,0:T(8,128)} copy(f32[48,128,256]{2,0,1:T(8,128)S(1)} %convolution_add_fusion) | data formatting | bytes 12582912 | tf_op jit(solution)/shard_map/add | solution.py:17
  126.7 230.4 %reduce-scatter.3.cloned.1.call-done = f32[128,256]{1,0:T(8,128)} async-done(((f32[6144,256]{1,0:T(8,128)}), f32[128,256]{1,0:T(8,128)}) %reduce-scatter.3.cloned.1.call-update) | async-done | bytes 131088 | tf_op jit(solution)/shard_map/reduce_scatter | solution.py:50
  357.1 1.7 multiply_convert_fusion.1
  358.9 1.7 convolution_convert_fusion
  360.6 107.7 %all-gather.5.cloned.1.call-done = bf16[6144,256]{1,0:T(8,128)(2,1)} async-done(((bf16[128,256]{1,0:T(8,128)(2,1)}), bf16[6144,256]{1,0:T(8,128)(2,1)}) %all-gather.5.cloned.1.call-update) | async-done | bytes 3145744 | tf_op jit(solution)/shard_map/all_gather | solution.py:55
  468.3 2.6 gather_fusion.1
  470.9 3.0 fusion
  473.9 3.4 copy.28
  477.4 4.6 copy.29
  482.4 1.1 copy-done.1
  483.5 0.5 add_convert_fusion
  484.0 1.3 copy.30
  485.3 87.2 %reduce-scatter.5.cloned.1.call-done = bf16[128,256]{1,0:T(8,128)(2,1)} async-done(((bf16[2048,256]{1,0:T(8,128)(2,1)}), bf16[128,256]{1,0:T(8,128)(2,1)}) %reduce-scatter.5.cloned.1.call-update) | async-done | bytes 65552 | tf_op jit(solution)/shard_map/reduce_scatter | solution.py:66
  (23 shorter events, 0.7 us)
Async XLA Ops:
  7.2 99.5 %copy-start = (bf16[1,1,32,128,128]{4,3,2,1,0:T(8,128)(2,1)S(1)}, bf16[1,1,32,128,128]{4,3,2,1,0:T(8,128)(2,1)}, u32[]{:S(2)}) copy-start(bf16[1,1,32,128,128]{4,3,2,1,0:T(8,128)(2,1)} %param.8) | copy-start | bytes 3145732
  7.2 97.5 %all-gather.3.cloned.1.call-start = ((), (), s32[]{:S(2)}) async-start(), calls=%async_computation.2 | async-start | bytes 1114112 | tf_op jit(solution)/shard_map/all_gather | solution.py:40
  7.9 349.2 %reduce-scatter.3.cloned.1.call-start = ((), (), s32[]{:S(2)}) async-start(), calls=%async_computation.3 | async-start | bytes 6422528 | tf_op jit(solution)/shard_map/reduce_scatter | solution.py:50
  113.1 4.6 copy-start.3
  117.6 1.6 copy-start.2
  126.6 230.5 %copy-start.5 = (bf16[256,256]{1,0:T(8,128)(2,1)S(1)}, bf16[256,256]{1,0:T(8,128)(2,1)}, u32[]{:S(2)}) copy-start(bf16[256,256]{1,0:T(8,128)(2,1)} %param.12) | copy-start | bytes 393220
  126.6 341.7 %all-gather.5.cloned.1.call-start = ((), (), s32[]{:S(2)}) async-start(), calls=%async_computation.4 | async-start | bytes 3211264 | tf_op jit(solution)/shard_map/all_gather | solution.py:55
  360.6 212.0 %reduce-scatter.5.cloned.1.call-start = ((), (), s32[]{:S(2)}) async-start(), calls=%async_computation.5 | async-start | bytes 1114112 | tf_op jit(solution)/shard_map/reduce_scatter | solution.py:66
  477.3 4.6 copy-start.4
  481.9 1.6 copy-start.1
Sparse Core Ops, SparseCore 0:
  10.4 94.2 all-gather.2
  126.8 230.3 reduce-scatter.2
  361.7 106.5 all-gather.4
  485.5 87.0 reduce-scatter.4
where the time goes:
time: 580 us; the launch traced here: 579 us
  waiting for transfers between devices  521 us (90%)
  local copies, waits for them, and re-layouts  29.7 us (5%)
  between operations  14.6 us (3%)
  matrix products  12.5 us (2%)
    reduce_scatter x1, waiting for transfers between devices, per_device(): lax.psum_scatter(partial_value, ('col', 'rep'), scatter_dimension=0, tile...  230 us
    all_gather x1, waiting for transfers between devices, per_device(): grad_rows = lax.all_gather(grad_piece, ('col', 'rep'), axis=0, tiled=True)  108 us
    all_gather x1, waiting for transfers between devices, per_device(): panels = lax.all_gather(features, 'row', axis=0, tiled=True)  94.8 us
    reduce_scatter x1, waiting for transfers between devices, per_device(): lax.psum_scatter(column_part.astype(jnp.bfloat16), 'row', scatter_dimensi...  87.2 us
  transfers between devices with their start and end apart: 4, of which 4 were waited for; matrix products, arithmetic and copies ran while one was open for 0% of the time, Pallas kernels for 0%

commit v1 on v0

v1 whole, which is shorter than its diff:
```python
import functools

import jax
import jax.numpy as jnp
from jax import lax
from jax.experimental import pallas as pl
from jax.experimental.pallas import tpu as pltpu
from jax.sharding import Mesh
from jax.sharding import PartitionSpec as P

TILE = 128
F = 256
X, ZL, Y, ZH, CORE = 4, 4, 8, 3, 2
ROWS = Y * ZH * CORE
COLS = X * ZL
BF = jnp.bfloat16
F32 = jnp.float32
UNROLL = 4


def forward_kernel(rows_ref, cols_ref, count_ref, adj_ref, panels_ref, out_ref, acc_ref):
    acc_ref[...] = jnp.zeros_like(acc_ref)

    def step(i, carry):
        products = []
        for k in range(UNROLL):
            t = i * UNROLL + k
            products.append(
                jnp.dot(adj_ref[t], panels_ref[cols_ref[t]], preferred_element_type=F32)
            )
        for k in range(UNROLL):
            row = rows_ref[i * UNROLL + k]
            acc_ref[row] += products[k]
        return carry

    lax.fori_loop(0, count_ref[0] // UNROLL, step, 0)

    def put(j, carry):
        for core in range(CORE):
            out_ref[core, j] = acc_ref[j * CORE + core].astype(BF)
        return carry

    lax.fori_loop(0, Y * ZH, put, 0)


def backward_kernel(rows_ref, cols_ref, count_ref, adj_ref, grads_ref, out_ref, acc_ref):
    acc_ref[...] = jnp.zeros_like(acc_ref)

    def step(i, carry):
        products = []
        for k in range(UNROLL):
            t = i * UNROLL + k
            row = rows_ref[t]
            grad = grads_ref[row % CORE, row // CORE]
            products.append(
                lax.dot_general(
                    adj_ref[t], grad, (((0,), (0,)), ((), ())), preferred_element_type=F32
                )
            )
        for k in range(UNROLL):
            acc_ref[cols_ref[i * UNROLL + k]] += products[k]
        return carry

    lax.fori_loop(0, count_ref[0] // UNROLL, step, 0)
    out_ref[...] = acc_ref[...].astype(BF)


def middle_kernel(parts_ref, weight_ref, cotangent_ref, layer_ref, grad_ref):
    summed = parts_ref[0].astype(F32)
    for k in range(1, ZH):
        summed = summed + parts_ref[k].astype(F32)
    weight = weight_ref[...]
    pre_act = jnp.dot(summed.astype(BF), weight, preferred_element_type=F32)
    sigma = jax.nn.sigmoid(pre_act)
    layer_ref[...] = (pre_act * sigma).astype(BF)
    grad_pre = (cotangent_ref[...].astype(F32) * sigma * (1.0 + pre_act * (1.0 - sigma))).astype(BF)
    grad_ref[...] = lax.dot_general(
        grad_pre, weight, (((1,), (1,)), ((), ())), preferred_element_type=F32
    ).astype(BF)


SMEM = pl.BlockSpec(memory_space=pltpu.SMEM)
VMEM = pl.BlockSpec(memory_space=pltpu.VMEM)
PARAMS = pltpu.CompilerParams(vmem_limit_bytes=40 * 2**20)


def slot_call(kernel, out_shape, acc_tiles):
    return pl.pallas_call(
        kernel,
        out_shape=jax.ShapeDtypeStruct(out_shape, BF),
        in_specs=[SMEM, SMEM, SMEM, VMEM, VMEM],
        out_specs=VMEM,
        scratch_shapes=[pltpu.VMEM((acc_tiles, TILE, F), F32)],
        compiler_params=PARAMS,
    )


def tile_exchange(x, axis):
    return lax.all_to_all(x, axis, 0, 0, tiled=True)


def gather_by_exchange(x, axis, n):
    return tile_exchange(jnp.broadcast_to(x[None], (n,) + x.shape), axis)


def tile_sum(x):
    return jnp.sum(x.astype(F32), axis=0)


def per_device(features, adj_tiles, tile_rows, tile_cols, tile_count, weight, cotangent):
    adj = adj_tiles[0, 0]
    rows = tile_rows[0, 0]
    cols = tile_cols[0, 0]
    count = tile_count[0]
    core = lax.axis_index("core")

    panels = gather_by_exchange(features[0], ("x", "zl"), COLS)
    partial = slot_call(forward_kernel, (CORE, Y * ZH, TILE, F), ROWS)(
        rows, cols, count, adj, panels
    )
    mine = lax.dynamic_index_in_dim(partial, core, 0, keepdims=False)
    theirs = lax.dynamic_index_in_dim(partial, 1 - core, 0, keepdims=False)
    got = lax.ppermute(theirs, "core", [(0, 1), (1, 0)])
    chip_sum = (mine.astype(F32) + got.astype(F32)).astype(BF)
    chip_sum = chip_sum.reshape(Y, ZH * TILE, F)
    y_sum = tile_sum(tile_exchange(chip_sum, "y")).astype(BF)
    parts = tile_exchange(y_sum.reshape(ZH, TILE, F), "zh")

    place = lax.axis_index(("y", "zh", "core"))
    own_grad = lax.dynamic_slice_in_dim(cotangent, place * TILE, TILE, 0)
    layer_out, grad_piece = pl.pallas_call(
        middle_kernel,
        out_shape=[jax.ShapeDtypeStruct((TILE, F), BF)] * 2,
        compiler_params=PARAMS,
    )(parts, weight, own_grad)

    grads = gather_by_exchange(grad_piece, "zh", ZH)
    grads = gather_by_exchange(grads.reshape(ZH * TILE, F), "y", Y)
    grads = grads.reshape(Y * ZH, TILE, F)
    grads = lax.all_gather(grads, "core", axis=0)
    column_part = slot_call(backward_kernel, (COLS, TILE, F), COLS)(
        rows, cols, count, adj, grads
    )
    grad_input = tile_sum(tile_exchange(column_part, ("x", "zl"))).astype(BF)
    return (layer_out, grad_input[None])


def solution(mesh):
    fine = Mesh(mesh.devices.reshape(X, ZL, Y, ZH, CORE), ("x", "zl", "y", "zh", "core"))
    row, sect = ("x", "zl"), ("y", "zh", "core")
    in_specs = (
        P(row, sect, None),
        P(row, sect, None, None, None),
        P(row, sect, None),
        P(row, sect, None),
        P(row, sect),
        P(),
        P(row, None),
    )
    out_specs = (P(row + sect, None), P(row, sect, None))
    return jax.shard_map(
        per_device, mesh=fine, in_specs=in_specs, out_specs=out_specs, check_vma=False
    )
```

time: 580 us -> 252 us (0.43)
  the two profiles are of different devices: /device:TPU:24 before, /device:TPU:8 now
where the time goes in v1:
time: 252 us; the launch traced here: 251 us
  blocking collectives  136 us (54%)
  waiting for transfers between devices  54.5 us (22%)
  starting transfers between devices  22.9 us (9%)
  between operations  14.8 us (6%)
  local copies, waits for them, and re-layouts  8.66 us (3%)
  Pallas kernels  7.57 us (3%)
  other arithmetic  6.82 us (3%)
    all_to_all x4, blocking collectives, tile_exchange(): return lax.all_to_all(x, axis, 0, 0, tiled=True)  136 us
    all_to_all x2, waiting for transfers between devices, tile_exchange(): return lax.all_to_all(x, axis, 0, 0, tiled=True)  36.3 us
    all_to_all x2, starting transfers between devices, tile_exchange(): return lax.all_to_all(x, axis, 0, 0, tiled=True)  21 us
    all_gather x1, waiting for transfers between devices, per_device(): grads = lax.all_gather(grads, 'core', axis=0)  14.5 us
  transfers between devices with their start and end apart: 4, of which 4 were waited for; matrix products, arithmetic and copies ran while one was open for 0% of the time, Pallas kernels for 0%

profile of v1, /device:TPU:8, one launch (start us, length us, event | category | flops | bytes accessed | tf_op | source)
XLA Modules:
  0.0 251.2 jit_solution(5437305506378989844)
XLA Ops:
  7.2 2.1 broadcast_in_dim.24
  9.3 9.9 %all-to-all-start = ((bf16[16,128,256]{2,1,0:T(8,128)(2,1)}), bf16[16,128,256]{2,1,0:T(8,128)(2,1)}, u32[]{:S(2)}, u32[]{:S(2)}) async-start(bf16[16,128,256]{2,1,0:T(8,128)(2,1)} %broadcast_in_dim.24), calls=%async_computation | async-start | bytes 2097152 | tf_op jit(solution)/shard_map/all_to_all | solution.py:99
  19.8 27.2 %all-to-all-done.panels_ref = bf16[16,128,256]{2,1,0:T(8,128)(2,1)} async-done(((bf16[16,128,256]{2,1,0:T(8,128)(2,1)}), bf16[16,128,256]{2,1,0:T(8,128)(2,1)}, u32[]{:S(2)}, u32[]{:S(2)}) %all-to-all-start) | async-done | bytes 1048608 | tf_op jit(solution)/shard_map/all_to_all | solution.py:99
  47.0 1.2 copy-done.2
  48.2 3.9 %shard_map.86 = bf16[2,24,128,256]{3,2,1,0:T(8,128)(2,1)S(1)} custom-call(s32[32]{0:T(128)S(1)} %bitcast.19, s32[32]{0:T(128)S(1)} %bitcast.21, s32[1]{0:T(128)} %bitcast.15.count_ref, bf16[32,128,128]{2,1,0:T(8,128)(2,1)S(1)} %bitcast.17, bf16[16,128,256]{2,1,0:T(8,128)(2,1)} %all-to-all-done.panels_ref), custom_call_target="tpu_custom_call" | custom-call | tf_op jit(solution)/shard_map/pallas_call | solution.py:118
  52.1 1.5 dynamic-slice_bitcast_fusion
  53.6 0.6 copy-done.1
  54.2 1.9 collective-permute-start
  56.1 3.7 %collective-permute-done = bf16[24,128,256]{2,1,0:T(8,128)(2,1)} collective-permute-done((bf16[24,128,256]{2,1,0:T(8,128)(2,1)}, bf16[24,128,256]{2,1,0:T(8,128)(2,1)}, u32[]{:S(2)}, u32[]{:S(2)}) %collective-permute-start) | collective-permute-done | bytes 1572896 | tf_op jit(solution)/shard_map/ppermute | solution.py:123
  59.8 2.4 fusion
  62.3 45.5 %all_to_all.30 = bf16[8,384,256]{2,1,0:T(8,128)(2,1)} all-to-all(bf16[8,384,256]{2,1,0:T(8,128)(2,1)S(1)} %bitcast.24), channel_id=1, replica_groups=mesh['x'=4,'zl'=4,'y'=8,'zh'=3,'core'=2] {'y'}, dimensions={0} | all-to-all | bytes 3145728 | tf_op jit(solution)/shard_map/all_to_all | solution.py:99
  107.8 2.4 reduce_sum.24
  110.1 11.1 %all-to-all-start.2 = ((bf16[3,128,256]{2,1,0:T(8,128)(2,1)}), bf16[3,128,256]{2,1,0:T(8,128)(2,1)S(1)}, u32[]{:S(2)}, u32[]{:S(2)}) async-start(bf16[3,128,256]{2,1,0:T(8,128)(2,1)} %bitcast.26), calls=%async_computation.2 | async-start | bytes 393216 | tf_op jit(solution)/shard_map/all_to_all | solution.py:99
  121.2 9.1 %all-to-all-done.2.parts_ref = bf16[3,128,256]{2,1,0:T(8,128)(2,1)S(1)} async-done(((bf16[3,128,256]{2,1,0:T(8,128)(2,1)}), bf16[3,128,256]{2,1,0:T(8,128)(2,1)S(1)}, u32[]{:S(2)}, u32[]{:S(2)}) %all-to-all-start.2) | async-done | bytes 196640 | tf_op jit(solution)/shard_map/all_to_all | solution.py:99
  130.4 0.8 shard_map.87
  131.2 13.2 %all_to_all.31 = bf16[3,128,256]{2,1,0:T(8,128)(2,1)S(1)} all-to-all(bf16[3,128,256]{2,1,0:T(8,128)(2,1)S(1)} %broadcast_in_dim.25), channel_id=1, replica_groups=mesh['x'=4,'zl'=4,'y'=8,'zh'=3,'core'=2] {'zh'}, dimensions={0} | all-to-all | bytes 393216 | tf_op jit(solution)/shard_map/all_to_all | solution.py:99
  144.4 0.1 broadcast_in_dim.27
  144.5 41.6 %all_to_all.32 = bf16[8,384,256]{2,1,0:T(8,128)(2,1)} all-to-all(bf16[8,384,256]{2,1,0:T(8,128)(2,1)S(1)} %broadcast_in_dim.27), channel_id=1, replica_groups=mesh['x'=4,'zl'=4,'y'=8,'zh'=3,'core'=2] {'y'}, dimensions={0} | all-to-all | bytes 3145728 | tf_op jit(solution)/shard_map/all_to_all | solution.py:99
  186.2 14.5 %all-gather.2.cloned.1.call-done.grads_ref = bf16[2,24,128,256]{3,2,1,0:T(8,128)(2,1)} async-done(((bf16[1,24,128,256]{3,2,1,0:T(8,128)(2,1)}), bf16[2,24,128,256]{3,2,1,0:T(8,128)(2,1)}) %all-gather.2.cloned.1.call-update) | async-done | bytes 3145744 | tf_op jit(solution)/shard_map/all_gather | solution.py:140
  200.7 1.2 copy-done.3
  201.9 1.9 copy-done.4
  203.8 2.9 %shard_map.88 = bf16[16,128,256]{2,1,0:T(8,128)(2,1)S(1)} custom-call(s32[32]{0:T(128)S(1)} %bitcast.20, s32[32]{0:T(128)S(1)} %bitcast.22, s32[1]{0:T(128)} %bitcast.16.count_ref, bf16[32,128,128]{2,1,0:T(8,128)(2,1)S(1)} %bitcast.18, bf16[2,24,128,256]{3,2,1,0:T(8,128)(2,1)S(1)} %copy-done.4), custom_call_target="tpu_custom_call" | custom-call | tf_op jit(solution)/shard_map/pallas_call | solution.py:141
  206.7 35.7 %all_to_all.33 = bf16[16,128,256]{2,1,0:T(8,128)(2,1)} all-to-all(bf16[16,128,256]{2,1,0:T(8,128)(2,1)S(1)} %shard_map.88), channel_id=1, replica_groups=mesh['x'=4,'zl'=4,'y'=8,'zh'=3,'core'=2] {'x','zl'}, dimensions={0} | all-to-all | bytes 2097152 | tf_op jit(solution)/shard_map/all_to_all | solution.py:99
  242.4 2.0 reduce_sum.25
  (16 shorter events, 0.1 us)
Async XLA Ops:
  7.2 114.1 %copy-start = (bf16[6144,256]{1,0:T(8,128)(2,1)S(1)}, bf16[6144,256]{1,0:T(8,128)(2,1)}, u32[]{:S(2)}) copy-start(bf16[6144,256]{1,0:T(8,128)(2,1)} %param.13) | copy-start | bytes 9437188
  7.2 39.8 %copy-start.6 = (s32[1,1,32]{2,1,0:T(1,128)S(1)}, s32[1,1,32]{2,1,0:T(1,128)}, u32[]{:S(2)}) copy-start(s32[1,1,32]{2,1,0:T(1,128)} %param.9) | copy-start | bytes 388
  7.2 39.8 %copy-start.7 = (s32[1,1,32]{2,1,0:T(1,128)S(1)}, s32[1,1,32]{2,1,0:T(1,128)}, u32[]{:S(2)}) copy-start(s32[1,1,32]{2,1,0:T(1,128)} %param.10) | copy-start | bytes 388
  9.3 37.7 %all-to-all-start = ((bf16[16,128,256]{2,1,0:T(8,128)(2,1)}), bf16[16,128,256]{2,1,0:T(8,128)(2,1)}, u32[]{:S(2)}, u32[]{:S(2)}) async-start(bf16[16,128,256]{2,1,0:T(8,128)(2,1)} %broadcast_in_dim.24), calls=%async_computation | async-start | bytes 2097152 | tf_op jit(solution)/shard_map/all_to_all | solution.py:99
  47.0 1.2 copy-start.2
  52.1 2.1 copy-start.1
  54.2 5.6 %collective-permute-start = (bf16[24,128,256]{2,1,0:T(8,128)(2,1)}, bf16[24,128,256]{2,1,0:T(8,128)(2,1)}, u32[]{:S(2)}, u32[]{:S(2)}) collective-permute-start(bf16[24,128,256]{2,1,0:T(8,128)(2,1)} %dynamic-slice_bitcast_fusion), channel_id=1, source_target_pairs={{0,1},{1,0},{2,3},{3,2},{4,5},{5,4},{6,7},{7,6},{8,9},{9,8},{10,11... | collective-permute-start | bytes 4718600 | tf_op jit(solution)/shard_map/ppermute | solution.py:123
  107.8 22.6 %copy-start.5 = (bf16[256,256]{1,0:T(8,128)(2,1)S(1)}, bf16[256,256]{1,0:T(8,128)(2,1)}, u32[]{:S(2)}) copy-start(bf16[256,256]{1,0:T(8,128)(2,1)} %weight_ref.1) | copy-start | bytes 393220
  110.1 20.2 %all-to-all-start.2 = ((bf16[3,128,256]{2,1,0:T(8,128)(2,1)}), bf16[3,128,256]{2,1,0:T(8,128)(2,1)S(1)}, u32[]{:S(2)}, u32[]{:S(2)}) async-start(bf16[3,128,256]{2,1,0:T(8,128)(2,1)} %bitcast.26), calls=%async_computation.2 | async-start | bytes 393216 | tf_op jit(solution)/shard_map/all_to_all | solution.py:99
  121.2 79.4 %all-gather.2.cloned.1.call-start = ((), (), s32[]{:S(2)}) async-start(), calls=%async_computation.6 | async-start | bytes 4718592 | tf_op jit(solution)/shard_map/all_gather | solution.py:140
  200.7 1.2 copy-start.3
  201.9 1.9 copy-start.4
Sparse Core Ops, SparseCore 0:
  186.3 14.3 all-gather.1

commit v2 on v1

v2 whole, which is shorter than its diff:
```python
import jax
import jax.numpy as jnp
from jax import lax
from jax.experimental import pallas as pl
from jax.experimental.pallas import tpu as pltpu
from jax.sharding import Mesh
from jax.sharding import PartitionSpec as P

TILE = 128
F = 256
X, ZL, Y, ZH, CORE = 4, 4, 8, 3, 2
COLS = X * ZL
HALF = Y * ZH
BF = jnp.bfloat16
F32 = jnp.float32
UNROLL = 4
GATHER_PLACE = (0, 2, 4, 7, 5, 6, 3, 1)


def forward_kernel(dst_ref, src_ref, count_ref, adj_ref, panels_ref, mine_ref, theirs_ref, acc_ref):
    acc_ref[...] = jnp.zeros_like(acc_ref)

    def step(i, carry):
        products = []
        for k in range(UNROLL):
            t = i * UNROLL + k
            products.append(
                jnp.dot(adj_ref[t], panels_ref[src_ref[t]], preferred_element_type=F32)
            )
        for k in range(UNROLL):
            acc_ref[dst_ref[i * UNROLL + k]] += products[k]
        return carry

    lax.fori_loop(0, count_ref[0] // UNROLL, step, 0)
    theirs_ref[...] = acc_ref[HALF:].astype(BF)
    mine_ref[...] = acc_ref[:HALF].astype(BF)


def backward_kernel(dst_ref, src_ref, count_ref, adj_ref, own_ref, other_ref, out_ref, acc_ref):
    acc_ref[...] = jnp.zeros_like(acc_ref)

    def step(i, carry):
        products = []
        for k in range(UNROLL):
            t = i * UNROLL + k
            src = src_ref[t]
            place = lax.rem(src, HALF)
            grad = jnp.where(src < HALF, own_ref[place], other_ref[place])
            products.append(
                lax.dot_general(
                    adj_ref[t], grad, (((0,), (0,)), ((), ())), preferred_element_type=F32
                )
            )
        for k in range(UNROLL):
            acc_ref[dst_ref[i * UNROLL + k]] += products[k]
        return carry

    lax.fori_loop(0, count_ref[0] // UNROLL, step, 0)
    out_ref[...] = acc_ref[...].astype(BF)


def middle_kernel(parts_ref, weight_ref, cotangent_ref, layer_ref, grad_ref):
    summed = parts_ref[0].astype(F32)
    for k in range(1, ZH):
        summed = summed + parts_ref[k].astype(F32)
    weight = weight_ref[...]
    pre_act = jnp.dot(summed.astype(BF), weight, preferred_element_type=F32)
    sigma = jax.nn.sigmoid(pre_act)
    layer_ref[...] = (pre_act * sigma).astype(BF)
    grad_pre = (cotangent_ref[...].astype(F32) * sigma * (1.0 + pre_act * (1.0 - sigma))).astype(BF)
    grad = lax.dot_general(
        grad_pre, weight, (((1,), (1,)), ((), ())), preferred_element_type=F32
    ).astype(BF)
    for k in range(ZH):
        grad_ref[k] = grad


SMEM = pl.BlockSpec(memory_space=pltpu.SMEM)
VMEM = pl.BlockSpec(memory_space=pltpu.VMEM)
PARAMS = pltpu.CompilerParams(vmem_limit_bytes=40 * 2**20)


def exchange(x, axis):
    return lax.all_to_all(x, axis, 0, 0, tiled=True)


def repeat(x, n):
    return jnp.broadcast_to(x[None], (n,) + x.shape)


def tile_sum(x):
    return jnp.sum(x.astype(F32), axis=0).astype(BF)


def add_up(*terms):
    total = terms[0].astype(F32)
    for term in terms[1:]:
        total = total + term.astype(F32)
    return total.astype(BF)


def swap_cores(x):
    return lax.ppermute(x, "core", [(0, 1), (1, 0)])


def shift(x, by):
    return lax.ppermute(x, "y", [(y, (y + by) % Y) for y in range(Y)])


def mirrored_shift(x, by):
    pairs = []
    for y in range(Y):
        pairs.append((y * CORE, (y + by) % Y * CORE))
        pairs.append((y * CORE + 1, (y - by) % Y * CORE + 1))
    return lax.ppermute(x, ("y", "core"), pairs)


def per_device(features, adj_tiles, tile_rows, tile_cols, tile_count, weight, cotangent):
    adj = adj_tiles[0, 0]
    rows = tile_rows[0, 0]
    cols = tile_cols[0, 0]
    count = tile_count[0]
    core = lax.axis_index("core")
    y = lax.axis_index("y")

    row_core = rows % CORE
    row_zh = rows // CORE % ZH
    row_ahead = (rows // (CORE * ZH) - y) % Y
    foreign = (row_core != core).astype(jnp.int32)
    steps = jnp.where(row_core == 0, row_ahead, (Y - row_ahead) % Y)
    sent_place = foreign * HALF + steps * ZH + row_zh
    gather_place = jnp.zeros_like(rows)
    for k, place in enumerate(GATHER_PLACE):
        gather_place = jnp.where(row_ahead == k, place, gather_place)
    gather_place = foreign * HALF + gather_place * ZH + row_zh

    panels = exchange(repeat(features[0], ZL), "zl")
    panels = exchange(repeat(panels, X), "x").reshape(COLS, TILE, F)
    mine, theirs = pl.pallas_call(
        forward_kernel,
        out_shape=[jax.ShapeDtypeStruct((HALF, TILE, F), BF)] * 2,
        in_specs=[SMEM, SMEM, SMEM, VMEM, VMEM],
        out_specs=[VMEM, VMEM],
        scratch_shapes=[pltpu.VMEM((CORE * HALF, TILE, F), F32)],
        compiler_params=PARAMS,
    )(sent_place, cols, count, adj, panels)
    chip = add_up(mine, swap_cores(theirs)).reshape(Y, ZH, TILE, F)
    from_four = mirrored_shift(chip[4], 2)
    from_three = mirrored_shift(chip[3], 1)
    from_minus_three = mirrored_shift(chip[5], -1)
    ones = [mirrored_shift(chip[1], 1), mirrored_shift(chip[7], -1)]
    minus_two = mirrored_shift(add_up(chip[6], from_minus_three), -2)
    plus_two = mirrored_shift(add_up(chip[2], from_four, from_three), 2)
    y_sum = add_up(chip[0], *ones, minus_two, plus_two)
    parts = exchange(y_sum, "zh")

    place = lax.axis_index(("y", "zh", "core"))
    own_grad = lax.dynamic_slice_in_dim(cotangent, place * TILE, TILE, 0)
    layer_out, grad_copies = pl.pallas_call(
        middle_kernel,
        out_shape=[
            jax.ShapeDtypeStruct((TILE, F), BF),
            jax.ShapeDtypeStruct((ZH, TILE, F), BF),
        ],
        compiler_params=PARAMS,
    )(parts, weight, own_grad)

    here = exchange(grad_copies, "zh")
    minus_one, plus_one = shift(here, 1), shift(here, -1)
    minus_two, plus_two = shift(here, 2), shift(here, -2)
    four = mirrored_shift(jnp.where(core == 0, minus_two, plus_two), 2)
    minus_three, plus_three = shift(minus_two, 1), shift(plus_two, -1)
    own = jnp.concatenate(
        [here, minus_one, plus_one, minus_two, plus_two, four, minus_three, plus_three]
    )
    other = swap_cores(own)
    column_part = pl.pallas_call(
        backward_kernel,
        out_shape=jax.ShapeDtypeStruct((COLS, TILE, F), BF),
        in_specs=[SMEM, SMEM, SMEM, VMEM, VMEM, VMEM],
        out_specs=VMEM,
        scratch_shapes=[pltpu.VMEM((COLS, TILE, F), F32)],
        compiler_params=PARAMS,
    )(cols, gather_place, count, adj, own, other)
    x_sum = tile_sum(exchange(column_part.reshape(X, ZL, TILE, F), "x"))
    grad_input = tile_sum(exchange(x_sum, "zl"))
    return (layer_out, grad_input[None])


def solution(mesh):
    fine = Mesh(mesh.devices.reshape(X, ZL, Y, ZH, CORE), ("x", "zl", "y", "zh", "core"))
    row, sect = ("x", "zl"), ("y", "zh", "core")
    in_specs = (
        P(row, sect, None),
        P(row, sect, None, None, None),
        P(row, sect, None),
        P(row, sect, None),
        P(row, sect),
        P(),
        P(row, None),
    )
    out_specs = (P(row + sect, None), P(row, sect, None))
    return jax.shard_map(
        per_device, mesh=fine, in_specs=in_specs, out_specs=out_specs, check_vma=False
    )
```

time: 252 us -> 200 us (0.79)
  the two profiles are of different devices: /device:TPU:8 before, /device:TPU:24 now
where the time goes in v2:
time: 200 us; the launch traced here: 199 us
  starting transfers between devices  64.4 us (32%)
  blocking collectives  59.9 us (30%)
  waiting for transfers between devices  57.9 us (29%)
  Pallas kernels  7.48 us (4%)
  other arithmetic  4.65 us (2%)
  local copies, waits for them, and re-layouts  3.5 us (2%)
    all_to_all x4, blocking collectives, exchange(): return lax.all_to_all(x, axis, 0, 0, tiled=True)  59.9 us
    ppermute x8, starting transfers between devices, mirrored_shift(): return lax.ppermute(x, ('y', 'core'), pairs)  25.2 us
    all_to_all x2, waiting for transfers between devices, exchange(): return lax.all_to_all(x, axis, 0, 0, tiled=True)  23.8 us
    ppermute x6, starting transfers between devices, shift(): return lax.ppermute(x, 'y', [(y, (y + by) % Y) for y in range(Y)])  20.3 us
    ppermute x6, waiting for transfers between devices, shift(): return lax.ppermute(x, 'y', [(y, (y + by) % Y) for y in range(Y)])  15.1 us
    all_to_all x2, starting transfers between devices, exchange(): return lax.all_to_all(x, axis, 0, 0, tiled=True)  15 us
    ppermute x8, waiting for transfers between devices, mirrored_shift(): return lax.ppermute(x, ('y', 'core'), pairs)  12.3 us
    ppermute x2, waiting for transfers between devices, swap_cores(): return lax.ppermute(x, 'core', [(0, 1), (1, 0)])  6.75 us
  transfers between devices with their start and end apart: 18, of which 12 were waited for; matrix products, arithmetic and copies ran while one was open for 0% of the time, Pallas kernels for 0%

profile of v2, /device:TPU:24, one launch (start us, length us, event | category | flops | bytes accessed | tf_op | source)
XLA Modules:
  0.0 199.3 jit_solution(7714112647375974138)
XLA Ops:
  1.7 15.9 %all_to_all.30 = bf16[4,128,256]{2,1,0:T(8,128)(2,1)S(1)} all-to-all(bf16[4,128,256]{2,1,0:T(8,128)(2,1)S(1)} %broadcast_in_dim.26), channel_id=1, replica_groups=mesh['x'=4,'zl'=4,'y'=8,'zh'=3,'core'=2] {'zl'}, dimensions={0} | all-to-all | bytes 524288 | tf_op jit(solution)/shard_map/all_to_all | solution.py:84
  18.7 4.3 %all-to-all-start.1 = ((bf16[4,4,128,256]{3,2,1,0:T(8,128)(2,1)}), bf16[4,4,128,256]{3,2,1,0:T(8,128)(2,1)}, u32[]{:S(2)}, u32[]{:S(2)}) async-start(bf16[4,4,128,256]{3,2,1,0:T(8,128)(2,1)} %broadcast_in_dim.27), calls=%async_computation.1 | async-start | bytes 2097152 | tf_op jit(solution)/shard_map/all_to_all | solution.py:84
  23.7 12.4 %all-to-all-done.1 = bf16[4,4,128,256]{3,2,1,0:T(8,128)(2,1)} async-done(((bf16[4,4,128,256]{3,2,1,0:T(8,128)(2,1)}), bf16[4,4,128,256]{3,2,1,0:T(8,128)(2,1)}, u32[]{:S(2)}, u32[]{:S(2)}) %all-to-all-start.1) | async-done | bytes 1048608 | tf_op jit(solution)/shard_map/all_to_all | solution.py:84
  37.3 3.8 %shard_map.86 = (bf16[24,128,256]{2,1,0:T(8,128)(2,1)S(1)}, bf16[24,128,256]{2,1,0:T(8,128)(2,1)S(1)}) custom-call(s32[32]{0:T(128)S(1)} %add_add_fusion.dst_ref, s32[32]{0:T(128)S(1)} %bitcast.43, s32[1]{0:T(128)} %bitcast.38.count_ref, bf16[32,128,128]{2,1,0:T(8,128)(2,1)S(1)} %bitcast.40, bf16[16,128,256]{2,1,0:T(8,128)(2,1)} %bitcast.5.panels_ref), custom_call_target="tpu_custom_call" | custom-call | tf_op jit(solution)/shard_map/pallas_call | solution.py:139
  43.0 3.4 %collective-permute-done = bf16[24,128,256]{2,1,0:T(8,128)(2,1)S(1)} collective-permute-done((bf16[24,128,256]{2,1,0:T(8,128)(2,1)S(1)}, bf16[24,128,256]{2,1,0:T(8,128)(2,1)S(1)}, u32[]{:S(2)}, u32[]{:S(2)}) %collective-permute-start) | collective-permute-done | bytes 1572896 | tf_op jit(solution)/shard_map/ppermute | solution.py:103
  49.1 4.8 %collective-permute-start.5 = (bf16[3,128,256]{2,1,0:T(8,128)(2,1)S(1)}, bf16[3,128,256]{2,1,0:T(8,128)(2,1)S(1)}, u32[]{:S(2)}, u32[]{:S(2)}) collective-permute-start(bf16[3,128,256]{2,1,0:T(8,128)(2,1)S(1)} %get-tuple-element.15), channel_id=1, source_target_pairs={{0,12},{1,37},{6,18},{7,43},{12,24},{13,1},{18,30},{19,7},{24,36},... | collective-permute-start | bytes 589832 | tf_op jit(solution)/shard_map/ppermute | solution.py:115
  53.9 2.6 %collective-permute-start.6 = (bf16[3,128,256]{2,1,0:T(8,128)(2,1)S(1)}, bf16[3,128,256]{2,1,0:T(8,128)(2,1)S(1)}, u32[]{:S(2)}, u32[]{:S(2)}) collective-permute-start(bf16[3,128,256]{2,1,0:T(8,128)(2,1)S(1)} %get-tuple-element.14), channel_id=1, source_target_pairs={{0,6},{1,43},{6,12},{7,1},{12,18},{13,7},{18,24},{19,13},{24,30},{... | collective-permute-start | bytes 589832 | tf_op jit(solution)/shard_map/ppermute | solution.py:115
  56.5 3.9 %collective-permute-start.1 = (bf16[3,128,256]{2,1,0:T(8,128)(2,1)S(1)}, bf16[3,128,256]{2,1,0:T(8,128)(2,1)S(1)}, u32[]{:S(2)}, u32[]{:S(2)}) collective-permute-start(bf16[3,128,256]{2,1,0:T(8,128)(2,1)S(1)} %get-tuple-element.13), channel_id=1, source_target_pairs={{0,6},{1,43},{6,12},{7,1},{12,18},{13,7},{18,24},{19,13},{24,30},{... | collective-permute-start | bytes 589832 | tf_op jit(solution)/shard_map/ppermute | solution.py:115
  64.2 2.8 %collective-permute-start.4 = (bf16[3,128,256]{2,1,0:T(8,128)(2,1)S(1)}, bf16[3,128,256]{2,1,0:T(8,128)(2,1)S(1)}, u32[]{:S(2)}, u32[]{:S(2)}) collective-permute-start(bf16[3,128,256]{2,1,0:T(8,128)(2,1)S(1)} %get-tuple-element.18), channel_id=1, source_target_pairs={{0,36},{1,13},{6,42},{7,19},{12,0},{13,25},{18,6},{19,31},{24,12},... | collective-permute-start | bytes 589832 | tf_op jit(solution)/shard_map/ppermute | solution.py:115
  67.0 5.1 %collective-permute-start.7 = (bf16[3,128,256]{2,1,0:T(8,128)(2,1)S(1)}, bf16[3,128,256]{2,1,0:T(8,128)(2,1)S(1)}, u32[]{:S(2)}, u32[]{:S(2)}) collective-permute-start(bf16[3,128,256]{2,1,0:T(8,128)(2,1)S(1)} %get-tuple-element.19), channel_id=1, source_target_pairs={{0,12},{1,37},{6,18},{7,43},{12,24},{13,1},{18,30},{19,7},{24,36},... | collective-permute-start | bytes 589832 | tf_op jit(solution)/shard_map/ppermute | solution.py:115
  72.2 7.7 %collective-permute-done.4 = bf16[3,128,256]{2,1,0:T(8,128)(2,1)S(1)} collective-permute-done((bf16[3,128,256]{2,1,0:T(8,128)(2,1)S(1)}, bf16[3,128,256]{2,1,0:T(8,128)(2,1)S(1)}, u32[]{:S(2)}, u32[]{:S(2)}) %collective-permute-start.4) | collective-permute-done | bytes 196640 | tf_op jit(solution)/shard_map/ppermute | solution.py:115
  80.7 10.8 %all-to-all-start.2 = ((bf16[3,128,256]{2,1,0:T(8,128)(2,1)}), bf16[3,128,256]{2,1,0:T(8,128)(2,1)S(1)}, u32[]{:S(2)}, u32[]{:S(2)}) async-start(bf16[3,128,256]{2,1,0:T(8,128)(2,1)} %add_convert_fusion.1), calls=%async_computation.2 | async-start | bytes 393216 | tf_op jit(solution)/shard_map/all_to_all | solution.py:84
  91.5 11.4 %all-to-all-done.2.parts_ref = bf16[3,128,256]{2,1,0:T(8,128)(2,1)S(1)} async-done(((bf16[3,128,256]{2,1,0:T(8,128)(2,1)}), bf16[3,128,256]{2,1,0:T(8,128)(2,1)S(1)}, u32[]{:S(2)}, u32[]{:S(2)}) %all-to-all-start.2) | async-done | bytes 196640 | tf_op jit(solution)/shard_map/all_to_all | solution.py:84
  103.6 12.3 %all_to_all.31 = bf16[3,128,256]{2,1,0:T(8,128)(2,1)S(1)} all-to-all(bf16[3,128,256]{2,1,0:T(8,128)(2,1)S(1)} %get-tuple-element.9), channel_id=1, replica_groups=mesh['x'=4,'zl'=4,'y'=8,'zh'=3,'core'=2] {'zh'}, dimensions={0} | all-to-all | bytes 393216 | tf_op jit(solution)/shard_map/all_to_all | solution.py:84
  115.9 4.6 %collective-permute-start.8 = (bf16[3,128,256]{2,1,0:T(8,128)(2,1)S(1)}, bf16[3,128,256]{2,1,0:T(8,128)(2,1)S(1)}, u32[]{:S(2)}, u32[]{:S(2)}) collective-permute-start(bf16[3,128,256]{2,1,0:T(8,128)(2,1)S(1)} %all_to_all.31), channel_id=1, source_target_pairs={{0,6},{6,12},{12,18},{18,24},{24,30},{30,36},{36,42},{42,0},{1,7},... | collective-permute-start | bytes 589832 | tf_op jit(solution)/shard_map/ppermute | solution.py:107
  122.4 4.4 %collective-permute-start.10 = (bf16[3,128,256]{2,1,0:T(8,128)(2,1)S(1)}, bf16[3,128,256]{2,1,0:T(8,128)(2,1)S(1)}, u32[]{:S(2)}, u32[]{:S(2)}) collective-permute-start(bf16[3,128,256]{2,1,0:T(8,128)(2,1)S(1)} %all_to_all.31), channel_id=1, source_target_pairs={{0,12},{6,18},{12,24},{18,30},{24,36},{30,42},{36,0},{42,6},{1,13}... | collective-permute-start | bytes 589832 | tf_op jit(solution)/shard_map/ppermute | solution.py:107
  130.1 3.9 %collective-permute-done.10 = bf16[3,128,256]{2,1,0:T(8,128)(2,1)S(1)} collective-permute-done((bf16[3,128,256]{2,1,0:T(8,128)(2,1)S(1)}, bf16[3,128,256]{2,1,0:T(8,128)(2,1)S(1)}, u32[]{:S(2)}, u32[]{:S(2)}) %collective-permute-start.10) | collective-permute-done | bytes 196640 | tf_op jit(solution)/shard_map/ppermute | solution.py:107
  134.0 6.4 %collective-permute-done.11 = bf16[3,128,256]{2,1,0:T(8,128)(2,1)S(1)} collective-permute-done((bf16[3,128,256]{2,1,0:T(8,128)(2,1)S(1)}, bf16[3,128,256]{2,1,0:T(8,128)(2,1)S(1)}, u32[]{:S(2)}, u32[]{:S(2)}) %collective-permute-start.11) | collective-permute-done | bytes 196640 | tf_op jit(solution)/shard_map/ppermute | solution.py:107
  142.4 5.2 %collective-permute-start.13 = (bf16[3,128,256]{2,1,0:T(8,128)(2,1)S(1)}, bf16[3,128,256]{2,1,0:T(8,128)(2,1)S(1)}, u32[]{:S(2)}, u32[]{:S(2)}) collective-permute-start(bf16[3,128,256]{2,1,0:T(8,128)(2,1)S(1)} %collective-permute-done.10), channel_id=1, source_target_pairs={{0,6},{6,12},{12,18},{18,24},{24,30},{30,36},{36,42},{42,0},{1,7},... | collective-permute-start | bytes 589832 | tf_op jit(solution)/shard_map/ppermute | solution.py:107
  149.5 2.9 %collective-permute-done.12 = bf16[3,128,256]{2,1,0:T(8,128)(2,1)S(1)} collective-permute-done((bf16[3,128,256]{2,1,0:T(8,128)(2,1)S(1)}, bf16[3,128,256]{2,1,0:T(8,128)(2,1)S(1)}, u32[]{:S(2)}, u32[]{:S(2)}) %collective-permute-start.12) | collective-permute-done | bytes 196640 | tf_op jit(solution)/shard_map/ppermute | solution.py:115
  158.3 3.4 %collective-permute-done.15.other_ref = bf16[24,128,256]{2,1,0:T(8,128)(2,1)S(1)} collective-permute-done((bf16[24,128,256]{2,1,0:T(8,128)(2,1)S(1)}, bf16[24,128,256]{2,1,0:T(8,128)(2,1)S(1)}, u32[]{:S(2)}, u32[]{:S(2)}) %collective-permute-start.15) | collective-permute-done | bytes 1572896 | tf_op jit(solution)/shard_map/ppermute | solution.py:103
  161.7 2.9 %shard_map.88 = bf16[16,128,256]{2,1,0:T(8,128)(2,1)S(1)} custom-call(s32[32]{0:T(128)S(1)} %bitcast.44, s32[32]{0:T(128)S(1)} %get-tuple-element.10.src_ref, s32[1]{0:T(128)} %bitcast.39.count_ref, bf16[32,128,128]{2,1,0:T(8,128)(2,1)S(1)} %bitcast.41, bf16[24,128,256]{2,1,0:T(8,128)(2,1)S(1)} %constant_dynamic-update-slice_fusion.own_ref, ...), custom_call_target="tpu_custom_call" | custom-call | tf_op jit(solution)/shard_map/pallas_call | solution.py:177
  164.6 17.2 %all_to_all.32 = bf16[4,4,128,256]{3,2,1,0:T(8,128)(2,1)} all-to-all(bf16[4,4,128,256]{3,2,1,0:T(8,128)(2,1)S(1)} %bitcast.42), channel_id=1, replica_groups=mesh['x'=4,'zl'=4,'y'=8,'zh'=3,'core'=2] {'x'}, dimensions={0} | all-to-all | bytes 2097152 | tf_op jit(solution)/shard_map/all_to_all | solution.py:84
  183.2 14.5 %all_to_all.33 = bf16[4,128,256]{2,1,0:T(8,128)(2,1)} all-to-all(bf16[4,128,256]{2,1,0:T(8,128)(2,1)S(1)} %reduce_sum.24), channel_id=1, replica_groups=mesh['x'=4,'zl'=4,'y'=8,'zh'=3,'core'=2] {'zl'}, dimensions={0} | all-to-all | bytes 524288 | tf_op jit(solution)/shard_map/all_to_all | solution.py:84
  (50 shorter events, 31.4 us)
Async XLA Ops:
  0.6 90.8 %copy-start = (bf16[6144,256]{1,0:T(8,128)(2,1)S(1)}, bf16[6144,256]{1,0:T(8,128)(2,1)}, u32[]{:S(2)}) copy-start(bf16[6144,256]{1,0:T(8,128)(2,1)} %param.13) | copy-start | bytes 9437188
  17.6 6.0 %copy-start.5 = (s32[1,1,32]{2,1,0:T(1,128)S(1)}, s32[1,1,32]{2,1,0:T(1,128)}, u32[]{:S(2)}) copy-start(s32[1,1,32]{2,1,0:T(1,128)} %param.9) | copy-start | bytes 388
  17.6 18.5 %copy-start.4 = (s32[1,1,32]{2,1,0:T(1,128)S(1)}, s32[1,1,32]{2,1,0:T(1,128)}, u32[]{:S(2)}) copy-start(s32[1,1,32]{2,1,0:T(1,128)} %param.10) | copy-start | bytes 388
  18.7 17.4 %all-to-all-start.1 = ((bf16[4,4,128,256]{3,2,1,0:T(8,128)(2,1)}), bf16[4,4,128,256]{3,2,1,0:T(8,128)(2,1)}, u32[]{:S(2)}, u32[]{:S(2)}) async-start(bf16[4,4,128,256]{3,2,1,0:T(8,128)(2,1)} %broadcast_in_dim.27), calls=%async_computation.1 | async-start | bytes 2097152 | tf_op jit(solution)/shard_map/all_to_all | solution.py:84
  36.1 1.2 copy-start.1
  41.1 5.3 %collective-permute-start = (bf16[24,128,256]{2,1,0:T(8,128)(2,1)S(1)}, bf16[24,128,256]{2,1,0:T(8,128)(2,1)S(1)}, u32[]{:S(2)}, u32[]{:S(2)}) collective-permute-start(bf16[24,128,256]{2,1,0:T(8,128)(2,1)S(1)} %get-tuple-element.7), channel_id=1, source_target_pairs={{0,1},{1,0},{2,3},{3,2},{4,5},{5,4},{6,7},{7,6},{8,9},{9,8},{10,11... | collective-permute-start | bytes 4718600 | tf_op jit(solution)/shard_map/ppermute | solution.py:103
  47.0 55.8 %copy-start.3 = (bf16[256,256]{1,0:T(8,128)(2,1)S(1)}, bf16[256,256]{1,0:T(8,128)(2,1)}, u32[]{:S(2)}) copy-start(bf16[256,256]{1,0:T(8,128)(2,1)} %weight_ref.1) | copy-start | bytes 393220
  47.0 15.3 %collective-permute-start.3 = (bf16[3,128,256]{2,1,0:T(8,128)(2,1)S(1)}, bf16[3,128,256]{2,1,0:T(8,128)(2,1)S(1)}, u32[]{:S(2)}, u32[]{:S(2)}) collective-permute-start(bf16[3,128,256]{2,1,0:T(8,128)(2,1)S(1)} %get-tuple-element.16), channel_id=1, source_target_pairs={{0,42},{1,7},{6,0},{7,13},{12,6},{13,19},{18,12},{19,25},{24,18},{... | collective-permute-start | bytes 589832 | tf_op jit(solution)/shard_map/ppermute | solution.py:115
  49.1 13.3 %collective-permute-start.5 = (bf16[3,128,256]{2,1,0:T(8,128)(2,1)S(1)}, bf16[3,128,256]{2,1,0:T(8,128)(2,1)S(1)}, u32[]{:S(2)}, u32[]{:S(2)}) collective-permute-start(bf16[3,128,256]{2,1,0:T(8,128)(2,1)S(1)} %get-tuple-element.15), channel_id=1, source_target_pairs={{0,12},{1,37},{6,18},{7,43},{12,24},{13,1},{18,30},{19,7},{24,36},... | collective-permute-start | bytes 589832 | tf_op jit(solution)/shard_map/ppermute | solution.py:115
  53.9 10.2 %collective-permute-start.6 = (bf16[3,128,256]{2,1,0:T(8,128)(2,1)S(1)}, bf16[3,128,256]{2,1,0:T(8,128)(2,1)S(1)}, u32[]{:S(2)}, u32[]{:S(2)}) collective-permute-start(bf16[3,128,256]{2,1,0:T(8,128)(2,1)S(1)} %get-tuple-element.14), channel_id=1, source_target_pairs={{0,6},{1,43},{6,12},{7,1},{12,18},{13,7},{18,24},{19,13},{24,30},{... | collective-permute-start | bytes 589832 | tf_op jit(solution)/shard_map/ppermute | solution.py:115
  56.5 15.7 %collective-permute-start.1 = (bf16[3,128,256]{2,1,0:T(8,128)(2,1)S(1)}, bf16[3,128,256]{2,1,0:T(8,128)(2,1)S(1)}, u32[]{:S(2)}, u32[]{:S(2)}) collective-permute-start(bf16[3,128,256]{2,1,0:T(8,128)(2,1)S(1)} %get-tuple-element.13), channel_id=1, source_target_pairs={{0,6},{1,43},{6,12},{7,1},{12,18},{13,7},{18,24},{19,13},{24,30},{... | collective-permute-start | bytes 589832 | tf_op jit(solution)/shard_map/ppermute | solution.py:115
  60.4 11.7 %collective-permute-start.2 = (bf16[3,128,256]{2,1,0:T(8,128)(2,1)S(1)}, bf16[3,128,256]{2,1,0:T(8,128)(2,1)S(1)}, u32[]{:S(2)}, u32[]{:S(2)}) collective-permute-start(bf16[3,128,256]{2,1,0:T(8,128)(2,1)S(1)} %get-tuple-element.17), channel_id=1, source_target_pairs={{0,42},{1,7},{6,0},{7,13},{12,6},{13,19},{18,12},{19,25},{24,18},{... | collective-permute-start | bytes 589832 | tf_op jit(solution)/shard_map/ppermute | solution.py:115
  64.2 15.7 %collective-permute-start.4 = (bf16[3,128,256]{2,1,0:T(8,128)(2,1)S(1)}, bf16[3,128,256]{2,1,0:T(8,128)(2,1)S(1)}, u32[]{:S(2)}, u32[]{:S(2)}) collective-permute-start(bf16[3,128,256]{2,1,0:T(8,128)(2,1)S(1)} %get-tuple-element.18), channel_id=1, source_target_pairs={{0,36},{1,13},{6,42},{7,19},{12,0},{13,25},{18,6},{19,31},{24,12},... | collective-permute-start | bytes 589832 | tf_op jit(solution)/shard_map/ppermute | solution.py:115
  67.0 12.9 %collective-permute-start.7 = (bf16[3,128,256]{2,1,0:T(8,128)(2,1)S(1)}, bf16[3,128,256]{2,1,0:T(8,128)(2,1)S(1)}, u32[]{:S(2)}, u32[]{:S(2)}) collective-permute-start(bf16[3,128,256]{2,1,0:T(8,128)(2,1)S(1)} %get-tuple-element.19), channel_id=1, source_target_pairs={{0,12},{1,37},{6,18},{7,43},{12,24},{13,1},{18,30},{19,7},{24,36},... | collective-permute-start | bytes 589832 | tf_op jit(solution)/shard_map/ppermute | solution.py:115
  80.7 22.1 %all-to-all-start.2 = ((bf16[3,128,256]{2,1,0:T(8,128)(2,1)}), bf16[3,128,256]{2,1,0:T(8,128)(2,1)S(1)}, u32[]{:S(2)}, u32[]{:S(2)}) async-start(bf16[3,128,256]{2,1,0:T(8,128)(2,1)} %add_convert_fusion.1), calls=%async_computation.2 | async-start | bytes 393216 | tf_op jit(solution)/shard_map/all_to_all | solution.py:84
  115.9 13.3 %collective-permute-start.8 = (bf16[3,128,256]{2,1,0:T(8,128)(2,1)S(1)}, bf16[3,128,256]{2,1,0:T(8,128)(2,1)S(1)}, u32[]{:S(2)}, u32[]{:S(2)}) collective-permute-start(bf16[3,128,256]{2,1,0:T(8,128)(2,1)S(1)} %all_to_all.31), channel_id=1, source_target_pairs={{0,6},{6,12},{12,18},{18,24},{24,30},{30,36},{36,42},{42,0},{1,7},... | collective-permute-start | bytes 589832 | tf_op jit(solution)/shard_map/ppermute | solution.py:107
  120.5 9.6 %collective-permute-start.9 = (bf16[3,128,256]{2,1,0:T(8,128)(2,1)S(1)}, bf16[3,128,256]{2,1,0:T(8,128)(2,1)S(1)}, u32[]{:S(2)}, u32[]{:S(2)}) collective-permute-start(bf16[3,128,256]{2,1,0:T(8,128)(2,1)S(1)} %all_to_all.31), channel_id=1, source_target_pairs={{0,42},{6,0},{12,6},{18,12},{24,18},{30,24},{36,30},{42,36},{1,43}... | collective-permute-start | bytes 589832 | tf_op jit(solution)/shard_map/ppermute | solution.py:107
  122.4 11.6 %collective-permute-start.10 = (bf16[3,128,256]{2,1,0:T(8,128)(2,1)S(1)}, bf16[3,128,256]{2,1,0:T(8,128)(2,1)S(1)}, u32[]{:S(2)}, u32[]{:S(2)}) collective-permute-start(bf16[3,128,256]{2,1,0:T(8,128)(2,1)S(1)} %all_to_all.31), channel_id=1, source_target_pairs={{0,12},{6,18},{12,24},{18,30},{24,36},{30,42},{36,0},{42,6},{1,13}... | collective-permute-start | bytes 589832 | tf_op jit(solution)/shard_map/ppermute | solution.py:107
  126.8 13.6 %collective-permute-start.11 = (bf16[3,128,256]{2,1,0:T(8,128)(2,1)S(1)}, bf16[3,128,256]{2,1,0:T(8,128)(2,1)S(1)}, u32[]{:S(2)}, u32[]{:S(2)}) collective-permute-start(bf16[3,128,256]{2,1,0:T(8,128)(2,1)S(1)} %all_to_all.31), channel_id=1, source_target_pairs={{0,36},{6,42},{12,0},{18,6},{24,12},{30,18},{36,24},{42,30},{1,37}... | collective-permute-start | bytes 589832 | tf_op jit(solution)/shard_map/ppermute | solution.py:107
  129.2 32.5 %copy-start.2 = (bf16[1,1,32,128,128]{4,3,2,1,0:T(8,128)(2,1)S(1)}, bf16[1,1,32,128,128]{4,3,2,1,0:T(8,128)(2,1)}, u32[]{:S(2)}) copy-start(bf16[1,1,32,128,128]{4,3,2,1,0:T(8,128)(2,1)} %param.8) | copy-start | bytes 3145732
  140.5 11.9 %collective-permute-start.12 = (bf16[3,128,256]{2,1,0:T(8,128)(2,1)S(1)}, bf16[3,128,256]{2,1,0:T(8,128)(2,1)S(1)}, u32[]{:S(2)}, u32[]{:S(2)}) collective-permute-start(bf16[3,128,256]{2,1,0:T(8,128)(2,1)S(1)} %get-tuple-element.20), channel_id=1, source_target_pairs={{0,12},{1,37},{6,18},{7,43},{12,24},{13,1},{18,30},{19,7},{24,36},... | collective-permute-start | bytes 589832 | tf_op jit(solution)/shard_map/ppermute | solution.py:115
  142.4 11.7 %collective-permute-start.13 = (bf16[3,128,256]{2,1,0:T(8,128)(2,1)S(1)}, bf16[3,128,256]{2,1,0:T(8,128)(2,1)S(1)}, u32[]{:S(2)}, u32[]{:S(2)}) collective-permute-start(bf16[3,128,256]{2,1,0:T(8,128)(2,1)S(1)} %collective-permute-done.10), channel_id=1, source_target_pairs={{0,6},{6,12},{12,18},{18,24},{24,30},{30,36},{36,42},{42,0},{1,7},... | collective-permute-start | bytes 589832 | tf_op jit(solution)/shard_map/ppermute | solution.py:107
  147.6 8.8 %collective-permute-start.14 = (bf16[3,128,256]{2,1,0:T(8,128)(2,1)S(1)}, bf16[3,128,256]{2,1,0:T(8,128)(2,1)S(1)}, u32[]{:S(2)}, u32[]{:S(2)}) collective-permute-start(bf16[3,128,256]{2,1,0:T(8,128)(2,1)S(1)} %collective-permute-done.11), channel_id=1, source_target_pairs={{0,42},{6,0},{12,6},{18,12},{24,18},{30,24},{36,30},{42,36},{1,43}... | collective-permute-start | bytes 589832 | tf_op jit(solution)/shard_map/ppermute | solution.py:107
  156.4 5.3 %collective-permute-start.15 = (bf16[24,128,256]{2,1,0:T(8,128)(2,1)S(1)}, bf16[24,128,256]{2,1,0:T(8,128)(2,1)S(1)}, u32[]{:S(2)}, u32[]{:S(2)}) collective-permute-start(bf16[24,128,256]{2,1,0:T(8,128)(2,1)S(1)} %constant_dynamic-update-slice_fusion.own_ref), channel_id=1, source_target_pairs={{0,1},{1,0},{2,3},{3,2},{4,5},{5,4},{6,7},{7,6},{8,9},{9,8},{10,11... | collective-permute-start | bytes 4718600 | tf_op jit(solution)/shard_map/ppermute | solution.py:103

commit v3 on v2

v3 whole, which is shorter than its diff:
```python
import jax
import jax.numpy as jnp
from jax import lax
from jax.experimental import pallas as pl
from jax.experimental.pallas import tpu as pltpu
from jax.sharding import Mesh
from jax.sharding import PartitionSpec as P

TILE = 128
F = 256
X, ZL, YH, YL, ZH, CORE = 4, 4, 4, 2, 3, 2
Y = YH * YL
COLS = X * ZL
HALF = Y * ZH
QUARTER = YH * ZH
BF = jnp.bfloat16
F32 = jnp.float32
UNROLL = 4


def pick_kernel(own_ref, cotangent_hbm, grads_ref, sems):
    copies = []
    for k in range(ZH):
        copies.append(
            pltpu.make_async_copy(
                cotangent_hbm.at[own_ref[0] + k * CORE], grads_ref.at[k], sems.at[k]
            )
        )
    for copy in copies:
        copy.start()
    for copy in copies:
        copy.wait()


def forward_kernel(
    dst_ref, src_ref, count_ref, adj_ref, panels_ref, mine_ref, theirs_ref, acc_ref
):
    acc_ref[...] = jnp.zeros_like(acc_ref)

    def step(i, carry):
        products = []
        for k in range(UNROLL):
            t = i * UNROLL + k
            products.append(
                jnp.dot(adj_ref[t], panels_ref[src_ref[t]], preferred_element_type=F32)
            )
        for k in range(UNROLL):
            acc_ref[dst_ref[i * UNROLL + k]] += products[k]
        return carry

    lax.fori_loop(0, count_ref[0] // UNROLL, step, 0)
    theirs_ref[...] = acc_ref[HALF:].astype(BF)
    mine_ref[...] = acc_ref[:HALF].astype(BF)

def backward_kernel(
    dst_ref, src_ref, count_ref, adj_ref, near_ref, far_ref, other_near_ref, other_far_ref,
    out_ref, acc_ref,
):
    acc_ref[...] = jnp.zeros_like(acc_ref)

    def step(i, carry):
        products = []
        for k in range(UNROLL):
            t = i * UNROLL + k
            src = src_ref[t]
            group = src // QUARTER
            place = src - group * QUARTER
            near = jnp.where(group < 2, near_ref[place], other_near_ref[place])
            far = jnp.where(group < 2, far_ref[place], other_far_ref[place])
            grad = jnp.where(lax.rem(group, 2) == 0, near, far)
            products.append(
                lax.dot_general(
                    adj_ref[t], grad, (((0,), (0,)), ((), ())), preferred_element_type=F32
                )
            )
        for k in range(UNROLL):
            acc_ref[dst_ref[i * UNROLL + k]] += products[k]
        return carry

    lax.fori_loop(0, count_ref[0] // UNROLL, step, 0)
    out_ref[...] = acc_ref[...].astype(BF)


def middle_kernel(zh_ref, parts_ref, weight_ref, cotangent_ref, layer_ref, grad_ref, out_ref):
    summed = parts_ref[0].astype(F32)
    for k in range(1, ZH):
        summed = summed + parts_ref[k].astype(F32)
    summed = summed.reshape(ZH * TILE, F)
    weight = weight_ref[...]
    pre_act = jnp.dot(summed.astype(BF), weight, preferred_element_type=F32)
    sigma = jax.nn.sigmoid(pre_act)
    out_ref[...] = (pre_act * sigma).reshape(ZH, TILE, F)
    layer_ref[...] = out_ref[zh_ref[0]].astype(BF)
    cotangent = cotangent_ref[...].reshape(ZH * TILE, F).astype(F32)
    grad_pre = (cotangent * sigma * (1.0 + pre_act * (1.0 - sigma))).astype(BF)
    grad = lax.dot_general(
        grad_pre, weight, (((1,), (1,)), ((), ())), preferred_element_type=F32
    ).astype(BF)
    grad_ref[...] = grad.reshape(ZH, TILE, F)


SMEM = pl.BlockSpec(memory_space=pltpu.SMEM)
VMEM = pl.BlockSpec(memory_space=pltpu.VMEM)
HBM = pl.BlockSpec(memory_space=pl.ANY)


def params(mib):
    return pltpu.CompilerParams(vmem_limit_bytes=mib * 2**20)


def exchange(x, axis):
    return lax.all_to_all(x, axis, 0, 0, tiled=True)


def repeat(x, n):
    return jnp.broadcast_to(x[None], (n,) + x.shape)


def tile_sum(x):
    return jnp.sum(x.astype(F32), axis=0).astype(BF)


def add_up(*terms):
    total = terms[0].astype(F32)
    for term in terms[1:]:
        total = total + term.astype(F32)
    return total.astype(BF)


def swap_cores(x):
    return lax.ppermute(x, "core", [(0, 1), (1, 0)])


def mirrored_shift(x, by):
    pairs = []
    for y in range(Y):
        pairs.append((y * CORE, (y + by) % Y * CORE))
        pairs.append((y * CORE + 1, (y - by) % Y * CORE + 1))
    return lax.ppermute(x, ("yh", "yl", "core"), pairs)


def neighbour_exchange(x):
    pairs = []
    for y in range(Y):
        up = 1 if y % 2 == 0 else -1
        pairs.append((y * CORE, (y + up) % Y * CORE))
        pairs.append((y * CORE + 1, (y - up) % Y * CORE + 1))
    return lax.ppermute(x, ("yh", "yl", "core"), pairs)


def per_device(features, adj_tiles, tile_rows, tile_cols, tile_count, weight, cotangent):
    adj = adj_tiles[0, 0]
    rows = tile_rows[0, 0]
    cols = tile_cols[0, 0]
    count = tile_count[0]
    core = lax.axis_index("core")
    y = lax.axis_index(("yh", "yl"))

    row_core = rows % CORE
    row_zh = rows // CORE % ZH
    row_y = rows // (CORE * ZH)
    row_ahead = (row_y - y) % Y
    foreign = (row_core != core).astype(jnp.int32)
    steps = jnp.where(row_core == 0, row_ahead, (Y - row_ahead) % Y)
    sent_place = foreign * HALF + steps * ZH + row_zh
    gather_place = foreign * HALF + (row_ahead % 2) * QUARTER + row_y // YL * ZH + row_zh

    panels = exchange(repeat(features[0], ZL), "zl")
    panels = exchange(repeat(panels, X), "x").reshape(COLS, TILE, F)
    tiles = cotangent.reshape(HALF * CORE, TILE, F)
    first_own = y * (ZH * CORE) + core
    own_grads = pl.pallas_call(
        pick_kernel,
        out_shape=jax.ShapeDtypeStruct((ZH, TILE, F), BF),
        in_specs=[SMEM, HBM],
        out_specs=VMEM,
        scratch_shapes=[pltpu.SemaphoreType.DMA((ZH,))],
        compiler_params=params(4),
    )(first_own[None], tiles)
    panels, own_grads = lax.optimization_barrier((panels, own_grads))
    mine, theirs = pl.pallas_call(
        forward_kernel,
        out_shape=[
            jax.ShapeDtypeStruct((HALF, TILE, F), BF),
            jax.ShapeDtypeStruct((HALF, TILE, F), BF),
        ],
        in_specs=[SMEM, SMEM, SMEM, VMEM, VMEM],
        out_specs=[VMEM, VMEM],
        scratch_shapes=[pltpu.VMEM((CORE * HALF, TILE, F), F32)],
        compiler_params=params(18),
    )(sent_place, cols, count, adj, panels)
    chip = add_up(mine, swap_cores(theirs)).reshape(Y, ZH, TILE, F)
    from_four = mirrored_shift(chip[4], 2)
    from_three = mirrored_shift(chip[3], 1)
    from_minus_three = mirrored_shift(chip[5], -1)
    ones = [mirrored_shift(chip[1], 1), mirrored_shift(chip[7], -1)]
    minus_two = mirrored_shift(add_up(chip[6], from_minus_three), -2)
    plus_two = mirrored_shift(add_up(chip[2], from_four, from_three), 2)
    y_sum = add_up(chip[0], *ones, minus_two, plus_two)
    parts = lax.all_gather(y_sum, "zh", axis=0)

    layer_out, here = pl.pallas_call(
        middle_kernel,
        out_shape=[
            jax.ShapeDtypeStruct((TILE, F), BF),
            jax.ShapeDtypeStruct((ZH, TILE, F), BF),
        ],
        in_specs=[SMEM, VMEM, VMEM, VMEM],
        out_specs=[VMEM, VMEM],
        scratch_shapes=[pltpu.VMEM((ZH, TILE, F), F32)],
        compiler_params=params(8),
    )(lax.axis_index("zh")[None], parts, weight, own_grads)

    near = lax.all_gather(here, "yh", axis=0).reshape(QUARTER, TILE, F)
    far = neighbour_exchange(near)
    other_near, other_far = swap_cores(near), swap_cores(far)
    column_part = pl.pallas_call(
        backward_kernel,
        out_shape=jax.ShapeDtypeStruct((COLS, TILE, F), BF),
        in_specs=[SMEM] * 3 + [VMEM] * 5,
        out_specs=VMEM,
        scratch_shapes=[pltpu.VMEM((COLS, TILE, F), F32)],
        compiler_params=params(14),
    )(cols, gather_place, count, adj, near, far, other_near, other_far)
    x_sum = tile_sum(exchange(column_part.reshape(X, ZL, TILE, F), "x"))
    grad_input = tile_sum(exchange(x_sum, "zl"))
    return (layer_out, grad_input[None])


def solution(mesh):
    fine = Mesh(
        mesh.devices.reshape(X, ZL, YH, YL, ZH, CORE), ("x", "zl", "yh", "yl", "zh", "core")
    )
    row, sect = ("x", "zl"), ("yh", "yl", "zh", "core")
    in_specs = (
        P(row, sect, None),
        P(row, sect, None, None, None),
        P(row, sect, None),
        P(row, sect, None),
        P(row, sect),
        P(),
        P(row, None),
    )
    out_specs = (P(row + sect, None), P(row, sect, None))
    return jax.shard_map(
        per_device, mesh=fine, in_specs=in_specs, out_specs=out_specs, check_vma=False
    )
```

time: 200 us -> 186 us (0.930)
  the two profiles are of different devices: /device:TPU:24 before, /device:TPU:2 now
where the time goes in v3:
time: 186 us; the launch traced here: 185 us
  blocking collectives  99.2 us (53%)
  starting transfers between devices  38.8 us (21%)
  waiting for transfers between devices  29.8 us (16%)
  Pallas kernels  7.22 us (4%)
  local copies, waits for them, and re-layouts  5.04 us (3%)
  other arithmetic  3.43 us (2%)
    all_to_all x3, blocking collectives, exchange(): return lax.all_to_all(x, axis, 0, 0, tiled=True)  47.3 us
    all_gather x1, blocking collectives, per_device(): parts = lax.all_gather(y_sum, 'zh', axis=0)  33.1 us
    ppermute x7, starting transfers between devices, mirrored_shift(): return lax.ppermute(x, ('yh', 'yl', 'core'), pairs)  24.5 us
    all_gather x1, blocking collectives, per_device(): near = lax.all_gather(here, 'yh', axis=0).reshape(QUARTER, TILE, F)  18.8 us
    ppermute x1, waiting for transfers between devices, neighbour_exchange(): return lax.ppermute(x, ('yh', 'yl', 'core'), pairs)  10 us
    ppermute x7, waiting for transfers between devices, mirrored_shift(): return lax.ppermute(x, ('yh', 'yl', 'core'), pairs)  7.79 us
    all_to_all x1, starting transfers between devices, exchange(): return lax.all_to_all(x, axis, 0, 0, tiled=True)  6.61 us
    all_to_all x1, waiting for transfers between devices, exchange(): return lax.all_to_all(x, axis, 0, 0, tiled=True)  6.32 us
  transfers between devices with their start and end apart: 12, of which 6 were waited for; matrix products, arithmetic and copies ran while one was open for 1% of the time, Pallas kernels for 0%

profile of v3, /device:TPU:2, one launch (start us, length us, event | category | flops | bytes accessed | tf_op | source)
XLA Modules:
  0.0 184.9 jit_solution(3551484257644148258)
XLA Ops:
  1.5 15.9 %all_to_all.20 = bf16[4,128,256]{2,1,0:T(8,128)(2,1)S(1)} all-to-all(bf16[4,128,256]{2,1,0:T(8,128)(2,1)S(1)} %broadcast_in_dim.24), channel_id=1, replica_groups=mesh['x'=4,'zl'=4,'yh'=4,'yl'=2,'zh'=3,'core'=2] {'zl'}, dimensions={0} | all-to-all | bytes 524288 | tf_op jit(solution)/shard_map/all_to_all | solution.py:112
  18.5 6.6 %all-to-all-start.1 = ((bf16[4,4,128,256]{3,2,1,0:T(8,128)(2,1)}), bf16[4,4,128,256]{3,2,1,0:T(8,128)(2,1)S(1)}, u32[]{:S(2)}, u32[]{:S(2)}) async-start(bf16[4,4,128,256]{3,2,1,0:T(8,128)(2,1)} %broadcast_in_dim.25), calls=%async_computation.1 | async-start | bytes 2097152 | tf_op jit(solution)/shard_map/all_to_all | solution.py:112
  28.4 6.3 %all-to-all-done.1 = bf16[4,4,128,256]{3,2,1,0:T(8,128)(2,1)S(1)} async-done(((bf16[4,4,128,256]{3,2,1,0:T(8,128)(2,1)}), bf16[4,4,128,256]{3,2,1,0:T(8,128)(2,1)S(1)}, u32[]{:S(2)}, u32[]{:S(2)}) %all-to-all-start.1) | async-done | bytes 1048608 | tf_op jit(solution)/shard_map/all_to_all | solution.py:112
  34.7 3.1 %shard_map.87 = (bf16[24,128,256]{2,1,0:T(8,128)(2,1)S(1)}, bf16[24,128,256]{2,1,0:T(8,128)(2,1)S(1)}) custom-call(s32[32]{0:T(128)S(1)} %add_add_fusion.dst_ref, s32[32]{0:T(128)S(1)} %bitcast.45, s32[1]{0:T(128)} %bitcast.37.count_ref, bf16[32,128,128]{2,1,0:T(8,128)(2,1)S(1)} %bitcast.40, bf16[16,128,256]{2,1,0:T(8,128)(2,1)S(1)} %bitcast.39), custom_call_target="tpu_custom_call" | custom-call | tf_op jit(solution)/shard_map/pallas_call | solution.py:181
  37.8 1.9 %collective-permute-start = (bf16[24,128,256]{2,1,0:T(8,128)(2,1)S(1)}, bf16[24,128,256]{2,1,0:T(8,128)(2,1)S(1)}, u32[]{:S(2)}, u32[]{:S(2)}) collective-permute-start(bf16[24,128,256]{2,1,0:T(8,128)(2,1)S(1)} %get-tuple-element.10), channel_id=1, source_target_pairs={{0,1},{1,0},{2,3},{3,2},{4,5},{5,4},{6,7},{7,6},{8,9},{9,8},{10,11... | collective-permute-start | bytes 4718600 | tf_op jit(solution)/shard_map/ppermute | solution.py:131
  39.8 3.4 %collective-permute-done = bf16[24,128,256]{2,1,0:T(8,128)(2,1)S(1)} collective-permute-done((bf16[24,128,256]{2,1,0:T(8,128)(2,1)S(1)}, bf16[24,128,256]{2,1,0:T(8,128)(2,1)S(1)}, u32[]{:S(2)}, u32[]{:S(2)}) %collective-permute-start) | collective-permute-done | bytes 1572896 | tf_op jit(solution)/shard_map/ppermute | solution.py:131
  44.5 2.5 %collective-permute-start.6 = (bf16[3,128,256]{2,1,0:T(8,128)(2,1)S(1)}, bf16[3,128,256]{2,1,0:T(8,128)(2,1)S(1)}, u32[]{:S(2)}, u32[]{:S(2)}) collective-permute-start(bf16[3,128,256]{2,1,0:T(8,128)(2,1)S(1)} %get-tuple-element.18), channel_id=1, source_target_pairs={{0,6},{1,43},{6,12},{7,1},{12,18},{13,7},{18,24},{19,13},{24,30},{... | collective-permute-start | bytes 589832 | tf_op jit(solution)/shard_map/ppermute | solution.py:139
  47.1 4.0 %collective-permute-start.5 = (bf16[3,128,256]{2,1,0:T(8,128)(2,1)S(1)}, bf16[3,128,256]{2,1,0:T(8,128)(2,1)S(1)}, u32[]{:S(2)}, u32[]{:S(2)}) collective-permute-start(bf16[3,128,256]{2,1,0:T(8,128)(2,1)S(1)} %get-tuple-element.19), channel_id=1, source_target_pairs={{0,12},{1,37},{6,18},{7,43},{12,24},{13,1},{18,30},{19,7},{24,36},... | collective-permute-start | bytes 589832 | tf_op jit(solution)/shard_map/ppermute | solution.py:139
  51.1 4.0 %collective-permute-start.3 = (bf16[3,128,256]{2,1,0:T(8,128)(2,1)S(1)}, bf16[3,128,256]{2,1,0:T(8,128)(2,1)S(1)}, u32[]{:S(2)}, u32[]{:S(2)}) collective-permute-start(bf16[3,128,256]{2,1,0:T(8,128)(2,1)S(1)} %get-tuple-element.20), channel_id=1, source_target_pairs={{0,42},{1,7},{6,0},{7,13},{12,6},{13,19},{18,12},{19,25},{24,18},{... | collective-permute-start | bytes 589832 | tf_op jit(solution)/shard_map/ppermute | solution.py:139
  55.1 2.6 %collective-permute-start.1 = (bf16[3,128,256]{2,1,0:T(8,128)(2,1)}, bf16[3,128,256]{2,1,0:T(8,128)(2,1)S(1)}, u32[]{:S(2)}, u32[]{:S(2)}) collective-permute-start(bf16[3,128,256]{2,1,0:T(8,128)(2,1)} %get-tuple-element.17), channel_id=1, source_target_pairs={{0,6},{1,43},{6,12},{7,1},{12,18},{13,7},{18,24},{19,13},{24,30},{... | collective-permute-start | bytes 589832 | tf_op jit(solution)/shard_map/ppermute | solution.py:139
  57.7 4.6 %collective-permute-start.2 = (bf16[3,128,256]{2,1,0:T(8,128)(2,1)}, bf16[3,128,256]{2,1,0:T(8,128)(2,1)S(1)}, u32[]{:S(2)}, u32[]{:S(2)}) collective-permute-start(bf16[3,128,256]{2,1,0:T(8,128)(2,1)} %get-tuple-element.21), channel_id=1, source_target_pairs={{0,42},{1,7},{6,0},{7,13},{12,6},{13,19},{18,12},{19,25},{24,18},{... | collective-permute-start | bytes 589832 | tf_op jit(solution)/shard_map/ppermute | solution.py:139
  63.3 3.0 %collective-permute-start.4 = (bf16[3,128,256]{2,1,0:T(8,128)(2,1)}, bf16[3,128,256]{2,1,0:T(8,128)(2,1)S(1)}, u32[]{:S(2)}, u32[]{:S(2)}) collective-permute-start(bf16[3,128,256]{2,1,0:T(8,128)(2,1)} %get-tuple-element.22), channel_id=1, source_target_pairs={{0,36},{1,13},{6,42},{7,19},{12,0},{13,25},{18,6},{19,31},{24,12},... | collective-permute-start | bytes 589832 | tf_op jit(solution)/shard_map/ppermute | solution.py:139
  66.3 3.7 %collective-permute-start.7 = (bf16[3,128,256]{2,1,0:T(8,128)(2,1)}, bf16[3,128,256]{2,1,0:T(8,128)(2,1)}, u32[]{:S(2)}, u32[]{:S(2)}) collective-permute-start(bf16[3,128,256]{2,1,0:T(8,128)(2,1)} %get-tuple-element.23), channel_id=1, source_target_pairs={{0,12},{1,37},{6,18},{7,43},{12,24},{13,1},{18,30},{19,7},{24,36},... | collective-permute-start | bytes 589832 | tf_op jit(solution)/shard_map/ppermute | solution.py:139
  70.0 7.5 %collective-permute-done.4 = bf16[3,128,256]{2,1,0:T(8,128)(2,1)S(1)} collective-permute-done((bf16[3,128,256]{2,1,0:T(8,128)(2,1)}, bf16[3,128,256]{2,1,0:T(8,128)(2,1)S(1)}, u32[]{:S(2)}, u32[]{:S(2)}) %collective-permute-start.4) | collective-permute-done | bytes 196640 | tf_op jit(solution)/shard_map/ppermute | solution.py:139
  78.9 33.1 %all-gather = bf16[9,128,256]{2,1,0:T(8,128)(2,1)S(1)} all-gather(bf16[3,128,256]{2,1,0:T(8,128)(2,1)S(1)} %add_convert_fusion.1), channel_id=2, replica_groups=mesh['x'=4,'zl'=4,'yh'=4,'yl'=2,'zh'=3,'core'=2] {'zh'}, dimensions={0}, use_global_device_ids=true | all-gather | bytes 786432 | tf_op jit(solution)/shard_map/all_gather | solution.py:200
  113.0 18.8 %all-gather.1.near_ref = bf16[12,128,256]{2,1,0:T(8,128)(2,1)S(1)} all-gather(bf16[3,128,256]{2,1,0:T(8,128)(2,1)S(1)} %get-tuple-element.13), channel_id=3, replica_groups=mesh['x'=4,'zl'=4,'yh'=4,'yl'=2,'zh'=3,'core'=2] {'yh'}, dimensions={0}, use_global_device_ids=true | all-gather | bytes 983040 | tf_op jit(solution)/shard_map/all_gather | solution.py:214
  131.7 1.9 %collective-permute-start.8 = (bf16[12,128,256]{2,1,0:T(8,128)(2,1)S(1)}, bf16[12,128,256]{2,1,0:T(8,128)(2,1)S(1)}, u32[]{:S(2)}, u32[]{:S(2)}) collective-permute-start(bf16[12,128,256]{2,1,0:T(8,128)(2,1)S(1)} %all-gather.1.near_ref), channel_id=1, source_target_pairs={{0,6},{1,43},{6,0},{7,13},{12,18},{13,7},{18,12},{19,25},{24,30},{... | collective-permute-start | bytes 2359304 | tf_op jit(solution)/shard_map/ppermute | solution.py:148
  133.7 1.9 %collective-permute-start.9 = (bf16[12,128,256]{2,1,0:T(8,128)(2,1)S(1)}, bf16[12,128,256]{2,1,0:T(8,128)(2,1)S(1)}, u32[]{:S(2)}, u32[]{:S(2)}) collective-permute-start(bf16[12,128,256]{2,1,0:T(8,128)(2,1)S(1)} %all-gather.1.near_ref), channel_id=1, source_target_pairs={{0,1},{1,0},{2,3},{3,2},{4,5},{5,4},{6,7},{7,6},{8,9},{9,8},{10,11... | collective-permute-start | bytes 2359304 | tf_op jit(solution)/shard_map/ppermute | solution.py:131
  135.6 10.0 %collective-permute-done.8.far_ref = bf16[12,128,256]{2,1,0:T(8,128)(2,1)S(1)} collective-permute-done((bf16[12,128,256]{2,1,0:T(8,128)(2,1)S(1)}, bf16[12,128,256]{2,1,0:T(8,128)(2,1)S(1)}, u32[]{:S(2)}, u32[]{:S(2)}) %collective-permute-start.8) | collective-permute-done | bytes 786464 | tf_op jit(solution)/shard_map/ppermute | solution.py:148
  145.6 1.9 %collective-permute-start.10 = (bf16[12,128,256]{2,1,0:T(8,128)(2,1)S(1)}, bf16[12,128,256]{2,1,0:T(8,128)(2,1)S(1)}, u32[]{:S(2)}, u32[]{:S(2)}) collective-permute-start(bf16[12,128,256]{2,1,0:T(8,128)(2,1)S(1)} %collective-permute-done.8.far_ref), channel_id=1, source_target_pairs={{0,1},{1,0},{2,3},{3,2},{4,5},{5,4},{6,7},{7,6},{8,9},{9,8},{10,11... | collective-permute-start | bytes 2359304 | tf_op jit(solution)/shard_map/ppermute | solution.py:131
  147.5 2.2 %collective-permute-done.10.other_far_ref = bf16[12,128,256]{2,1,0:T(8,128)(2,1)S(1)} collective-permute-done((bf16[12,128,256]{2,1,0:T(8,128)(2,1)S(1)}, bf16[12,128,256]{2,1,0:T(8,128)(2,1)S(1)}, u32[]{:S(2)}, u32[]{:S(2)}) %collective-permute-start.10) | collective-permute-done | bytes 786464 | tf_op jit(solution)/shard_map/ppermute | solution.py:131
  149.8 2.9 %shard_map.89 = bf16[16,128,256]{2,1,0:T(8,128)(2,1)S(1)} custom-call(s32[32]{0:T(128)S(1)} %bitcast.46, s32[32]{0:T(128)S(1)} %get-tuple-element.14.src_ref, s32[1]{0:T(128)} %bitcast.38.count_ref, bf16[32,128,128]{2,1,0:T(8,128)(2,1)S(1)} %bitcast.41, bf16[12,128,256]{2,1,0:T(8,128)(2,1)S(1)} %all-gather.1.near_ref, ...), custom_call_target="tpu_custom_call" | custom-call | tf_op jit(solution)/shard_map/pallas_call | solution.py:217
  152.7 17.1 %all_to_all.21 = bf16[4,4,128,256]{3,2,1,0:T(8,128)(2,1)S(1)} all-to-all(bf16[4,4,128,256]{3,2,1,0:T(8,128)(2,1)S(1)} %bitcast.42), channel_id=1, replica_groups=mesh['x'=4,'zl'=4,'yh'=4,'yl'=2,'zh'=3,'core'=2] {'x'}, dimensions={0} | all-to-all | bytes 2097152 | tf_op jit(solution)/shard_map/all_to_all | solution.py:112
  170.0 14.3 %all_to_all.22 = bf16[4,128,256]{2,1,0:T(8,128)(2,1)S(1)} all-to-all(bf16[4,128,256]{2,1,0:T(8,128)(2,1)S(1)} %reduce_sum.24), channel_id=1, replica_groups=mesh['x'=4,'zl'=4,'yh'=4,'yl'=2,'zh'=3,'core'=2] {'zl'}, dimensions={0} | all-to-all | bytes 524288 | tf_op jit(solution)/shard_map/all_to_all | solution.py:112
  (29 shorter events, 10.0 us)
Async XLA Ops:
  18.5 16.2 %all-to-all-start.1 = ((bf16[4,4,128,256]{3,2,1,0:T(8,128)(2,1)}), bf16[4,4,128,256]{3,2,1,0:T(8,128)(2,1)S(1)}, u32[]{:S(2)}, u32[]{:S(2)}) async-start(bf16[4,4,128,256]{3,2,1,0:T(8,128)(2,1)} %broadcast_in_dim.25), calls=%async_computation.1 | async-start | bytes 2097152 | tf_op jit(solution)/shard_map/all_to_all | solution.py:112
  25.8 1.9 %copy-start.1 = (bf16[6144,256]{1,0:T(8,128)(2,1)S(1)}, bf16[6144,256]{1,0:T(8,128)(2,1)}, u32[]{:S(2)}) copy-start(bf16[6144,256]{1,0:T(8,128)(2,1)} %param.13) | copy-start | bytes 9437188
  27.7 0.7 copy-start.4
  27.7 7.0 %copy-start = (bf16[1,1,32,128,128]{4,3,2,1,0:T(8,128)(2,1)S(1)}, bf16[1,1,32,128,128]{4,3,2,1,0:T(8,128)(2,1)}, u32[]{:S(2)}) copy-start(bf16[1,1,32,128,128]{4,3,2,1,0:T(8,128)(2,1)} %param.8) | copy-start | bytes 3145732
  27.7 7.0 %copy-start.3 = (s32[1,1,32]{2,1,0:T(1,128)S(1)}, s32[1,1,32]{2,1,0:T(1,128)}, u32[]{:S(2)}) copy-start(s32[1,1,32]{2,1,0:T(1,128)} %param.10) | copy-start | bytes 388
  37.8 5.3 %collective-permute-start = (bf16[24,128,256]{2,1,0:T(8,128)(2,1)S(1)}, bf16[24,128,256]{2,1,0:T(8,128)(2,1)S(1)}, u32[]{:S(2)}, u32[]{:S(2)}) collective-permute-start(bf16[24,128,256]{2,1,0:T(8,128)(2,1)S(1)} %get-tuple-element.10), channel_id=1, source_target_pairs={{0,1},{1,0},{2,3},{3,2},{4,5},{5,4},{6,7},{7,6},{8,9},{9,8},{10,11... | collective-permute-start | bytes 4718600 | tf_op jit(solution)/shard_map/ppermute | solution.py:131
  44.5 17.8 %collective-permute-start.6 = (bf16[3,128,256]{2,1,0:T(8,128)(2,1)S(1)}, bf16[3,128,256]{2,1,0:T(8,128)(2,1)S(1)}, u32[]{:S(2)}, u32[]{:S(2)}) collective-permute-start(bf16[3,128,256]{2,1,0:T(8,128)(2,1)S(1)} %get-tuple-element.18), channel_id=1, source_target_pairs={{0,6},{1,43},{6,12},{7,1},{12,18},{13,7},{18,24},{19,13},{24,30},{... | collective-permute-start | bytes 589832 | tf_op jit(solution)/shard_map/ppermute | solution.py:139
  47.1 15.3 %collective-permute-start.5 = (bf16[3,128,256]{2,1,0:T(8,128)(2,1)S(1)}, bf16[3,128,256]{2,1,0:T(8,128)(2,1)S(1)}, u32[]{:S(2)}, u32[]{:S(2)}) collective-permute-start(bf16[3,128,256]{2,1,0:T(8,128)(2,1)S(1)} %get-tuple-element.19), channel_id=1, source_target_pairs={{0,12},{1,37},{6,18},{7,43},{12,24},{13,1},{18,30},{19,7},{24,36},... | collective-permute-start | bytes 589832 | tf_op jit(solution)/shard_map/ppermute | solution.py:139
  51.1 11.3 %collective-permute-start.3 = (bf16[3,128,256]{2,1,0:T(8,128)(2,1)S(1)}, bf16[3,128,256]{2,1,0:T(8,128)(2,1)S(1)}, u32[]{:S(2)}, u32[]{:S(2)}) collective-permute-start(bf16[3,128,256]{2,1,0:T(8,128)(2,1)S(1)} %get-tuple-element.20), channel_id=1, source_target_pairs={{0,42},{1,7},{6,0},{7,13},{12,6},{13,19},{18,12},{19,25},{24,18},{... | collective-permute-start | bytes 589832 | tf_op jit(solution)/shard_map/ppermute | solution.py:139
  55.1 14.9 %collective-permute-start.1 = (bf16[3,128,256]{2,1,0:T(8,128)(2,1)}, bf16[3,128,256]{2,1,0:T(8,128)(2,1)S(1)}, u32[]{:S(2)}, u32[]{:S(2)}) collective-permute-start(bf16[3,128,256]{2,1,0:T(8,128)(2,1)} %get-tuple-element.17), channel_id=1, source_target_pairs={{0,6},{1,43},{6,12},{7,1},{12,18},{13,7},{18,24},{19,13},{24,30},{... | collective-permute-start | bytes 589832 | tf_op jit(solution)/shard_map/ppermute | solution.py:139
  57.7 54.3 %copy-start.2 = (bf16[256,256]{1,0:T(8,128)(2,1)S(1)}, bf16[256,256]{1,0:T(8,128)(2,1)}, u32[]{:S(2)}) copy-start(bf16[256,256]{1,0:T(8,128)(2,1)} %weight_ref.1) | copy-start | bytes 393220
  57.7 12.3 %collective-permute-start.2 = (bf16[3,128,256]{2,1,0:T(8,128)(2,1)}, bf16[3,128,256]{2,1,0:T(8,128)(2,1)S(1)}, u32[]{:S(2)}, u32[]{:S(2)}) collective-permute-start(bf16[3,128,256]{2,1,0:T(8,128)(2,1)} %get-tuple-element.21), channel_id=1, source_target_pairs={{0,42},{1,7},{6,0},{7,13},{12,6},{13,19},{18,12},{19,25},{24,18},{... | collective-permute-start | bytes 589832 | tf_op jit(solution)/shard_map/ppermute | solution.py:139
  63.3 14.3 %collective-permute-start.4 = (bf16[3,128,256]{2,1,0:T(8,128)(2,1)}, bf16[3,128,256]{2,1,0:T(8,128)(2,1)S(1)}, u32[]{:S(2)}, u32[]{:S(2)}) collective-permute-start(bf16[3,128,256]{2,1,0:T(8,128)(2,1)} %get-tuple-element.22), channel_id=1, source_target_pairs={{0,36},{1,13},{6,42},{7,19},{12,0},{13,25},{18,6},{19,31},{24,12},... | collective-permute-start | bytes 589832 | tf_op jit(solution)/shard_map/ppermute | solution.py:139
  66.3 11.5 %collective-permute-start.7 = (bf16[3,128,256]{2,1,0:T(8,128)(2,1)}, bf16[3,128,256]{2,1,0:T(8,128)(2,1)}, u32[]{:S(2)}, u32[]{:S(2)}) collective-permute-start(bf16[3,128,256]{2,1,0:T(8,128)(2,1)} %get-tuple-element.23), channel_id=1, source_target_pairs={{0,12},{1,37},{6,18},{7,43},{12,24},{13,1},{18,30},{19,7},{24,36},... | collective-permute-start | bytes 589832 | tf_op jit(solution)/shard_map/ppermute | solution.py:139
  131.7 13.9 %collective-permute-start.8 = (bf16[12,128,256]{2,1,0:T(8,128)(2,1)S(1)}, bf16[12,128,256]{2,1,0:T(8,128)(2,1)S(1)}, u32[]{:S(2)}, u32[]{:S(2)}) collective-permute-start(bf16[12,128,256]{2,1,0:T(8,128)(2,1)S(1)} %all-gather.1.near_ref), channel_id=1, source_target_pairs={{0,6},{1,43},{6,0},{7,13},{12,18},{13,7},{18,12},{19,25},{24,30},{... | collective-permute-start | bytes 2359304 | tf_op jit(solution)/shard_map/ppermute | solution.py:148
  133.7 13.9 %collective-permute-start.9 = (bf16[12,128,256]{2,1,0:T(8,128)(2,1)S(1)}, bf16[12,128,256]{2,1,0:T(8,128)(2,1)S(1)}, u32[]{:S(2)}, u32[]{:S(2)}) collective-permute-start(bf16[12,128,256]{2,1,0:T(8,128)(2,1)S(1)} %all-gather.1.near_ref), channel_id=1, source_target_pairs={{0,1},{1,0},{2,3},{3,2},{4,5},{5,4},{6,7},{7,6},{8,9},{9,8},{10,11... | collective-permute-start | bytes 2359304 | tf_op jit(solution)/shard_map/ppermute | solution.py:131
  145.6 4.2 %collective-permute-start.10 = (bf16[12,128,256]{2,1,0:T(8,128)(2,1)S(1)}, bf16[12,128,256]{2,1,0:T(8,128)(2,1)S(1)}, u32[]{:S(2)}, u32[]{:S(2)}) collective-permute-start(bf16[12,128,256]{2,1,0:T(8,128)(2,1)S(1)} %collective-permute-done.8.far_ref), channel_id=1, source_target_pairs={{0,1},{1,0},{2,3},{3,2},{4,5},{5,4},{6,7},{7,6},{8,9},{9,8},{10,11... | collective-permute-start | bytes 2359304 | tf_op jit(solution)/shard_map/ppermute | solution.py:131

commit v4 on v3

--- a/solution.py
+++ b/solution.py
@@ -16,6 +16,7 @@
 BF = jnp.bfloat16
 F32 = jnp.float32
 UNROLL = 4
+SLOTS = 32
 
 
 def pick_kernel(own_ref, cotangent_hbm, grads_ref, sems):
@@ -32,8 +33,13 @@
         copy.wait()
 
 
+def repeat_kernel(x_ref, out_ref):
+    for k in range(X):
+        out_ref[k] = x_ref[...]
+
+
 def forward_kernel(
-    dst_ref, src_ref, count_ref, adj_ref, panels_ref, mine_ref, theirs_ref, acc_ref
+    plan_ref, adj_ref, panels_ref, mine_ref, theirs_ref, acc_ref
 ):
     acc_ref[...] = jnp.zeros_like(acc_ref)
 
@@ -42,19 +48,24 @@
         for k in range(UNROLL):
             t = i * UNROLL + k
             products.append(
-                jnp.dot(adj_ref[t], panels_ref[src_ref[t]], preferred_element_type=F32)
+                jnp.dot(adj_ref[t], panels_ref[plan_ref[2 * t + 1]], preferred_element_type=F32)
             )
         for k in range(UNROLL):
-            acc_ref[dst_ref[i * UNROLL + k]] += products[k]
+            acc_ref[plan_ref[2 * (i * UNROLL + k)]] += products[k]
         return carry
 
-    lax.fori_loop(0, count_ref[0] // UNROLL, step, 0)
+    lax.fori_loop(0, plan_ref[2 * SLOTS] // UNROLL, step, 0)
     theirs_ref[...] = acc_ref[HALF:].astype(BF)
     mine_ref[...] = acc_ref[:HALF].astype(BF)
 
+def chip_kernel(mine_ref, other_ref, *out_refs):
+    for k, out_ref in enumerate(out_refs):
+        at = slice(k * ZH, (k + 1) * ZH)
+        out_ref[...] = (mine_ref[at].astype(F32) + other_ref[at].astype(F32)).astype(BF)
+
+
 def backward_kernel(
-    dst_ref, src_ref, count_ref, adj_ref, near_ref, far_ref, other_near_ref, other_far_ref,
-    out_ref, acc_ref,
+    plan_ref, adj_ref, near_ref, far_ref, other_near_ref, other_far_ref, out_ref, acc_ref
 ):
     acc_ref[...] = jnp.zeros_like(acc_ref)
 
@@ -62,7 +73,7 @@
         products = []
         for k in range(UNROLL):
             t = i * UNROLL + k
-            src = src_ref[t]
+            src = plan_ref[2 * t + 1]
             group = src // QUARTER
             place = src - group * QUARTER
             near = jnp.where(group < 2, near_ref[place], other_near_ref[place])
@@ -74,10 +85,10 @@
                 )
             )
         for k in range(UNROLL):
-            acc_ref[dst_ref[i * UNROLL + k]] += products[k]
+            acc_ref[plan_ref[2 * (i * UNROLL + k)]] += products[k]
         return carry
 
-    lax.fori_loop(0, count_ref[0] // UNROLL, step, 0)
+    lax.fori_loop(0, plan_ref[2 * SLOTS] // UNROLL, step, 0)
     out_ref[...] = acc_ref[...].astype(BF)
 
 
@@ -148,6 +159,10 @@
     return lax.ppermute(x, ("yh", "yl", "core"), pairs)
 
 
+def slot_plan(targets, sources, count):
+    return jnp.concatenate([jnp.stack([targets, sources], axis=1).reshape(2 * SLOTS), count])
+
+
 def per_device(features, adj_tiles, tile_rows, tile_cols, tile_count, weight, cotangent):
     adj = adj_tiles[0, 0]
     rows = tile_rows[0, 0]
@@ -165,8 +180,18 @@
     sent_place = foreign * HALF + steps * ZH + row_zh
     gather_place = foreign * HALF + (row_ahead % 2) * QUARTER + row_y // YL * ZH + row_zh
 
-    panels = exchange(repeat(features[0], ZL), "zl")
-    panels = exchange(repeat(panels, X), "x").reshape(COLS, TILE, F)
+    forward_plan = slot_plan(sent_place, cols, count)
+    backward_plan = slot_plan(cols, gather_place, count)
+
+    panels = lax.all_gather(features[0], "zl", axis=0)
+    copies = pl.pallas_call(
+        repeat_kernel,
+        out_shape=jax.ShapeDtypeStruct((X, ZL, TILE, F), BF),
+        in_specs=[VMEM],
+        out_specs=VMEM,
+        compiler_params=params(6),
+    )(panels)
+    panels = exchange(copies, "x").reshape(COLS, TILE, F)
     tiles = cotangent.reshape(HALF * CORE, TILE, F)
     first_own = y * (ZH * CORE) + core
     own_grads = pl.pallas_call(
@@ -177,19 +202,25 @@
         scratch_shapes=[pltpu.SemaphoreType.DMA((ZH,))],
         compiler_params=params(4),
     )(first_own[None], tiles)
-    panels, own_grads = lax.optimization_barrier((panels, own_grads))
+    panels, own_grads, forward_plan, backward_plan = lax.optimization_barrier(
+        (panels, own_grads, forward_plan, backward_plan)
+    )
     mine, theirs = pl.pallas_call(
         forward_kernel,
         out_shape=[
             jax.ShapeDtypeStruct((HALF, TILE, F), BF),
             jax.ShapeDtypeStruct((HALF, TILE, F), BF),
         ],
-        in_specs=[SMEM, SMEM, SMEM, VMEM, VMEM],
+        in_specs=[SMEM, VMEM, VMEM],
         out_specs=[VMEM, VMEM],
         scratch_shapes=[pltpu.VMEM((CORE * HALF, TILE, F), F32)],
         compiler_params=params(18),
-    )(sent_place, cols, count, adj, panels)
-    chip = add_up(mine, swap_cores(theirs)).reshape(Y, ZH, TILE, F)
+    )(forward_plan, adj, panels)
+    chip = pl.pallas_call(
+        chip_kernel,
+        out_shape=[jax.ShapeDtypeStruct((ZH, TILE, F), BF)] * Y,
+        compiler_params=params(8),
+    )(mine, swap_cores(theirs))
     from_four = mirrored_shift(chip[4], 2)
     from_three = mirrored_shift(chip[3], 1)
     from_minus_three = mirrored_shift(chip[5], -1)
@@ -217,11 +248,11 @@
     column_part = pl.pallas_call(
         backward_kernel,
         out_shape=jax.ShapeDtypeStruct((COLS, TILE, F), BF),
-        in_specs=[SMEM] * 3 + [VMEM] * 5,
+        in_specs=[SMEM] + [VMEM] * 5,
         out_specs=VMEM,
         scratch_shapes=[pltpu.VMEM((COLS, TILE, F), F32)],
         compiler_params=params(14),
-    )(cols, gather_place, count, adj, near, far, other_near, other_far)
+    )(backward_plan, adj, near, far, other_near, other_far)
     x_sum = tile_sum(exchange(column_part.reshape(X, ZL, TILE, F), "x"))
     grad_input = tile_sum(exchange(x_sum, "zl"))
     return (layer_out, grad_input[None])

time: 186 us -> 184 us (0.989)
  starting transfers between devices: 38.8 us -> 48.1 us
  blocking collectives: 99.2 us -> 94.8 us
  local copies, waits for them, and re-layouts: 5.04 us -> 2.29 us
  other arithmetic: 3.43 us -> 1.29 us
  waiting for transfers between devices: 29.8 us -> 27.9 us
    all_gather x0 -> x1, blocking collectives: none -> 16.7 us  [per_device(): panels = lax.all_gather(features[0], 'zl', axis=0)]
    all_to_all x3 -> x2, blocking collectives: 47.3 us -> 33.6 us  [exchange(): return lax.all_to_all(x, axis, 0, 0, tiled=True)]
    all_gather x1, blocking collectives: 33.1 us -> 28.5 us  [per_device(): parts = lax.all_gather(y_sum, 'zh', axis=0)]
    ppermute x1, starting transfers between devices: 1.91 us -> 6.06 us  [neighbour_exchange(): return lax.ppermute(x, ('yh', 'yl', 'core'), pairs)]
    all_to_all x1, starting transfers between devices: 6.61 us -> 10.4 us  [exchange(): return lax.all_to_all(x, axis, 0, 0, tiled=True)]
    all_gather x1, blocking collectives: 18.8 us -> 16.1 us  [per_device(): near = lax.all_gather(here, 'yh', axis=0).reshape(QUARTER, TILE, F)]
    convert_element_type x3, other arithmetic: 2.5 us -> 0.27 us  [add_up(): return total.astype(BF)]
    ppermute x1, waiting for transfers between devices: 10 us -> 8.03 us  [neighbour_exchange(): return lax.ppermute(x, ('yh', 'yl', 'core'), pairs)]
  transfers between devices with their start and end apart: 12 -> 12, of which waited for: 6 -> 6; matrix products, arithmetic and copies ran while one was open for 1% -> 0% of each run, Pallas kernels for 0% -> 0%
where the time goes in v4:
time: 184 us; the launch traced here: 182 us
  blocking collectives  94.8 us (52%)
  starting transfers between devices  48.1 us (26%)
  waiting for transfers between devices  27.9 us (15%)
  Pallas kernels  6.62 us (4%)
  local copies, waits for them, and re-layouts  2.29 us (1%)
    all_to_all x2, blocking collectives, exchange(): return lax.all_to_all(x, axis, 0, 0, tiled=True)  33.6 us
    all_gather x1, blocking collectives, per_device(): parts = lax.all_gather(y_sum, 'zh', axis=0)  28.5 us
    ppermute x7, starting transfers between devices, mirrored_shift(): return lax.ppermute(x, ('yh', 'yl', 'core'), pairs)  25.8 us
    all_gather x1, blocking collectives, per_device(): panels = lax.all_gather(features[0], 'zl', axis=0)  16.7 us
    all_gather x1, blocking collectives, per_device(): near = lax.all_gather(here, 'yh', axis=0).reshape(QUARTER, TILE, F)  16.1 us
    all_to_all x1, starting transfers between devices, exchange(): return lax.all_to_all(x, axis, 0, 0, tiled=True)  10.4 us
    ppermute x7, waiting for transfers between devices, mirrored_shift(): return lax.ppermute(x, ('yh', 'yl', 'core'), pairs)  8.17 us
    ppermute x1, waiting for transfers between devices, neighbour_exchange(): return lax.ppermute(x, ('yh', 'yl', 'core'), pairs)  8.03 us
  transfers between devices with their start and end apart: 12, of which 6 were waited for; matrix products, arithmetic and copies ran while one was open for 0% of the time, Pallas kernels for 0%

profile of v4, /device:TPU:2, one launch (start us, length us, event | category | flops | bytes accessed | tf_op | source)
XLA Modules:
  0.0 182.5 jit_solution(4250670514092267343)
XLA Ops:
  0.6 16.7 %all_gather.15.x_ref = bf16[4,128,256]{2,1,0:T(8,128)(2,1)S(1)} all-gather(bf16[1,128,256]{2,1,0:T(8,128)(2,1)} %param.7), channel_id=1, replica_groups=mesh['x'=4,'zl'=4,'yh'=4,'yl'=2,'zh'=3,'core'=2] {'zl'}, dimensions={0}, use_global_device_ids=true | all-gather | bytes 327680 | tf_op jit(solution)/shard_map/all_gather | solution.py:186
  18.3 10.4 %all-to-all-start = ((bf16[4,4,128,256]{3,2,1,0:T(8,128)(2,1)}), bf16[4,4,128,256]{3,2,1,0:T(8,128)(2,1)S(1)}, u32[]{:S(2)}, u32[]{:S(2)}) async-start(bf16[4,4,128,256]{3,2,1,0:T(8,128)(2,1)} %shard_map.86), calls=%async_computation | async-start | bytes 2097152 | tf_op jit(solution)/shard_map/all_to_all | solution.py:123
  32.2 6.1 %all-to-all-done = bf16[4,4,128,256]{3,2,1,0:T(8,128)(2,1)S(1)} async-done(((bf16[4,4,128,256]{3,2,1,0:T(8,128)(2,1)}), bf16[4,4,128,256]{3,2,1,0:T(8,128)(2,1)S(1)}, u32[]{:S(2)}, u32[]{:S(2)}) %all-to-all-start) | async-done | bytes 1048608 | tf_op jit(solution)/shard_map/all_to_all | solution.py:123
  38.2 2.2 %shard_map.88 = (bf16[24,128,256]{2,1,0:T(8,128)(2,1)S(1)}, bf16[24,128,256]{2,1,0:T(8,128)(2,1)S(1)}) custom-call(s32[65]{0:T(128)S(1)} %get-tuple-element.18.plan_ref, bf16[32,128,128]{2,1,0:T(8,128)(2,1)S(1)} %bitcast.38, bf16[16,128,256]{2,1,0:T(8,128)(2,1)S(1)} %bitcast.37), custom_call_target="tpu_custom_call" | custom-call | tf_op jit(solution)/shard_map/pallas_call | solution.py:208
  40.4 1.9 %collective-permute-start = (bf16[24,128,256]{2,1,0:T(8,128)(2,1)S(1)}, bf16[24,128,256]{2,1,0:T(8,128)(2,1)S(1)}, u32[]{:S(2)}, u32[]{:S(2)}) collective-permute-start(bf16[24,128,256]{2,1,0:T(8,128)(2,1)S(1)} %get-tuple-element.21), channel_id=1, source_target_pairs={{0,1},{1,0},{2,3},{3,2},{4,5},{5,4},{6,7},{7,6},{8,9},{9,8},{10,11... | collective-permute-start | bytes 4718600 | tf_op jit(solution)/shard_map/ppermute | solution.py:142
  42.3 3.4 %collective-permute-done.other_ref = bf16[24,128,256]{2,1,0:T(8,128)(2,1)S(1)} collective-permute-done((bf16[24,128,256]{2,1,0:T(8,128)(2,1)S(1)}, bf16[24,128,256]{2,1,0:T(8,128)(2,1)S(1)}, u32[]{:S(2)}, u32[]{:S(2)}) %collective-permute-start) | collective-permute-done | bytes 1572896 | tf_op jit(solution)/shard_map/ppermute | solution.py:142
  46.1 1.9 %collective-permute-start.3 = (bf16[3,128,256]{2,1,0:T(8,128)(2,1)S(1)}, bf16[3,128,256]{2,1,0:T(8,128)(2,1)S(1)}, u32[]{:S(2)}, u32[]{:S(2)}) collective-permute-start(bf16[3,128,256]{2,1,0:T(8,128)(2,1)S(1)} %get-tuple-element.26), channel_id=1, source_target_pairs={{0,42},{1,7},{6,0},{7,13},{12,6},{13,19},{18,12},{19,25},{24,18},{... | collective-permute-start | bytes 589832 | tf_op jit(solution)/shard_map/ppermute | solution.py:150
  48.0 3.9 %collective-permute-start.1 = (bf16[3,128,256]{2,1,0:T(8,128)(2,1)S(1)}, bf16[3,128,256]{2,1,0:T(8,128)(2,1)S(1)}, u32[]{:S(2)}, u32[]{:S(2)}) collective-permute-start(bf16[3,128,256]{2,1,0:T(8,128)(2,1)S(1)} %get-tuple-element.23), channel_id=1, source_target_pairs={{0,6},{1,43},{6,12},{7,1},{12,18},{13,7},{18,24},{19,13},{24,30},{... | collective-permute-start | bytes 589832 | tf_op jit(solution)/shard_map/ppermute | solution.py:150
  51.9 3.1 %collective-permute-start.2 = (bf16[3,128,256]{2,1,0:T(8,128)(2,1)S(1)}, bf16[3,128,256]{2,1,0:T(8,128)(2,1)S(1)}, u32[]{:S(2)}, u32[]{:S(2)}) collective-permute-start(bf16[3,128,256]{2,1,0:T(8,128)(2,1)S(1)} %get-tuple-element.24), channel_id=1, source_target_pairs={{0,42},{1,7},{6,0},{7,13},{12,6},{13,19},{18,12},{19,25},{24,18},{... | collective-permute-start | bytes 589832 | tf_op jit(solution)/shard_map/ppermute | solution.py:150
  55.1 2.2 %collective-permute-start.5 = (bf16[3,128,256]{2,1,0:T(8,128)(2,1)S(1)}, bf16[3,128,256]{2,1,0:T(8,128)(2,1)S(1)}, u32[]{:S(2)}, u32[]{:S(2)}) collective-permute-start(bf16[3,128,256]{2,1,0:T(8,128)(2,1)S(1)} %get-tuple-element.28), channel_id=1, source_target_pairs={{0,12},{1,37},{6,18},{7,43},{12,24},{13,1},{18,30},{19,7},{24,36},... | collective-permute-start | bytes 589832 | tf_op jit(solution)/shard_map/ppermute | solution.py:150
  57.2 3.6 %collective-permute-start.6 = (bf16[3,128,256]{2,1,0:T(8,128)(2,1)S(1)}, bf16[3,128,256]{2,1,0:T(8,128)(2,1)S(1)}, u32[]{:S(2)}, u32[]{:S(2)}) collective-permute-start(bf16[3,128,256]{2,1,0:T(8,128)(2,1)S(1)} %get-tuple-element.29), channel_id=1, source_target_pairs={{0,6},{1,43},{6,12},{7,1},{12,18},{13,7},{18,24},{19,13},{24,30},{... | collective-permute-start | bytes 589832 | tf_op jit(solution)/shard_map/ppermute | solution.py:150
  60.9 4.9 %collective-permute-start.4 = (bf16[3,128,256]{2,1,0:T(8,128)(2,1)S(1)}, bf16[3,128,256]{2,1,0:T(8,128)(2,1)S(1)}, u32[]{:S(2)}, u32[]{:S(2)}) collective-permute-start(bf16[3,128,256]{2,1,0:T(8,128)(2,1)S(1)} %add_convert_fusion.2), channel_id=1, source_target_pairs={{0,36},{1,13},{6,42},{7,19},{12,0},{13,25},{18,6},{19,31},{24,12},... | collective-permute-start | bytes 589832 | tf_op jit(solution)/shard_map/ppermute | solution.py:150
  65.8 3.1 %collective-permute-done.6 = bf16[3,128,256]{2,1,0:T(8,128)(2,1)S(1)} collective-permute-done((bf16[3,128,256]{2,1,0:T(8,128)(2,1)S(1)}, bf16[3,128,256]{2,1,0:T(8,128)(2,1)S(1)}, u32[]{:S(2)}, u32[]{:S(2)}) %collective-permute-start.6) | collective-permute-done | bytes 196640 | tf_op jit(solution)/shard_map/ppermute | solution.py:150
  69.0 6.2 %collective-permute-start.7 = (bf16[3,128,256]{2,1,0:T(8,128)(2,1)S(1)}, bf16[3,128,256]{2,1,0:T(8,128)(2,1)S(1)}, u32[]{:S(2)}, u32[]{:S(2)}) collective-permute-start(bf16[3,128,256]{2,1,0:T(8,128)(2,1)S(1)} %add_convert_fusion.1), channel_id=1, source_target_pairs={{0,12},{1,37},{6,18},{7,43},{12,24},{13,1},{18,30},{19,7},{24,36},... | collective-permute-start | bytes 589832 | tf_op jit(solution)/shard_map/ppermute | solution.py:150
  75.3 5.1 %collective-permute-done.7 = bf16[3,128,256]{2,1,0:T(8,128)(2,1)S(1)} collective-permute-done((bf16[3,128,256]{2,1,0:T(8,128)(2,1)S(1)}, bf16[3,128,256]{2,1,0:T(8,128)(2,1)S(1)}, u32[]{:S(2)}, u32[]{:S(2)}) %collective-permute-start.7) | collective-permute-done | bytes 196640 | tf_op jit(solution)/shard_map/ppermute | solution.py:150
  80.5 28.5 %all-gather = bf16[9,128,256]{2,1,0:T(8,128)(2,1)S(1)} all-gather(bf16[3,128,256]{2,1,0:T(8,128)(2,1)S(1)} %add_convert_fusion), channel_id=2, replica_groups=mesh['x'=4,'zl'=4,'yh'=4,'yl'=2,'zh'=3,'core'=2] {'zh'}, dimensions={0}, use_global_device_ids=true | all-gather | bytes 786432 | tf_op jit(solution)/shard_map/all_gather | solution.py:231
  109.9 16.1 %all-gather.1.near_ref = bf16[12,128,256]{2,1,0:T(8,128)(2,1)S(1)} all-gather(bf16[3,128,256]{2,1,0:T(8,128)(2,1)S(1)} %get-tuple-element.33), channel_id=3, replica_groups=mesh['x'=4,'zl'=4,'yh'=4,'yl'=2,'zh'=3,'core'=2] {'yh'}, dimensions={0}, use_global_device_ids=true | all-gather | bytes 983040 | tf_op jit(solution)/shard_map/all_gather | solution.py:245
  125.9 6.1 %collective-permute-start.8 = (bf16[12,128,256]{2,1,0:T(8,128)(2,1)S(1)}, bf16[12,128,256]{2,1,0:T(8,128)(2,1)S(1)}, u32[]{:S(2)}, u32[]{:S(2)}) collective-permute-start(bf16[12,128,256]{2,1,0:T(8,128)(2,1)S(1)} %all-gather.1.near_ref), channel_id=1, source_target_pairs={{0,6},{1,43},{6,0},{7,13},{12,18},{13,7},{18,12},{19,25},{24,30},{... | collective-permute-start | bytes 2359304 | tf_op jit(solution)/shard_map/ppermute | solution.py:159
  132.0 1.9 %collective-permute-start.9 = (bf16[12,128,256]{2,1,0:T(8,128)(2,1)S(1)}, bf16[12,128,256]{2,1,0:T(8,128)(2,1)S(1)}, u32[]{:S(2)}, u32[]{:S(2)}) collective-permute-start(bf16[12,128,256]{2,1,0:T(8,128)(2,1)S(1)} %all-gather.1.near_ref), channel_id=1, source_target_pairs={{0,1},{1,0},{2,3},{3,2},{4,5},{5,4},{6,7},{7,6},{8,9},{9,8},{10,11... | collective-permute-start | bytes 2359304 | tf_op jit(solution)/shard_map/ppermute | solution.py:142
  133.9 8.0 %collective-permute-done.8.far_ref = bf16[12,128,256]{2,1,0:T(8,128)(2,1)S(1)} collective-permute-done((bf16[12,128,256]{2,1,0:T(8,128)(2,1)S(1)}, bf16[12,128,256]{2,1,0:T(8,128)(2,1)S(1)}, u32[]{:S(2)}, u32[]{:S(2)}) %collective-permute-start.8) | collective-permute-done | bytes 786464 | tf_op jit(solution)/shard_map/ppermute | solution.py:159
  142.0 1.9 %collective-permute-start.10 = (bf16[12,128,256]{2,1,0:T(8,128)(2,1)S(1)}, bf16[12,128,256]{2,1,0:T(8,128)(2,1)S(1)}, u32[]{:S(2)}, u32[]{:S(2)}) collective-permute-start(bf16[12,128,256]{2,1,0:T(8,128)(2,1)S(1)} %collective-permute-done.8.far_ref), channel_id=1, source_target_pairs={{0,1},{1,0},{2,3},{3,2},{4,5},{5,4},{6,7},{7,6},{8,9},{9,8},{10,11... | collective-permute-start | bytes 2359304 | tf_op jit(solution)/shard_map/ppermute | solution.py:142
  143.9 2.2 %collective-permute-done.10.other_far_ref = bf16[12,128,256]{2,1,0:T(8,128)(2,1)S(1)} collective-permute-done((bf16[12,128,256]{2,1,0:T(8,128)(2,1)S(1)}, bf16[12,128,256]{2,1,0:T(8,128)(2,1)S(1)}, u32[]{:S(2)}, u32[]{:S(2)}) %collective-permute-start.10) | collective-permute-done | bytes 786464 | tf_op jit(solution)/shard_map/ppermute | solution.py:142
  148.0 19.4 %all_to_all.15 = bf16[4,4,128,256]{3,2,1,0:T(8,128)(2,1)S(1)} all-to-all(bf16[4,4,128,256]{3,2,1,0:T(8,128)(2,1)S(1)} %bitcast.40), channel_id=1, replica_groups=mesh['x'=4,'zl'=4,'yh'=4,'yl'=2,'zh'=3,'core'=2] {'x'}, dimensions={0} | all-to-all | bytes 2097152 | tf_op jit(solution)/shard_map/all_to_all | solution.py:123
  167.6 14.2 %all_to_all.16 = bf16[4,128,256]{2,1,0:T(8,128)(2,1)S(1)} all-to-all(bf16[4,128,256]{2,1,0:T(8,128)(2,1)S(1)} %reduce_sum.24), channel_id=1, replica_groups=mesh['x'=4,'zl'=4,'yh'=4,'yl'=2,'zh'=3,'core'=2] {'zl'}, dimensions={0} | all-to-all | bytes 524288 | tf_op jit(solution)/shard_map/all_to_all | solution.py:123
  (34 shorter events, 8.1 us)
Async XLA Ops:
  17.3 12.2 %copy-start.3 = (s32[1,1,32]{2,1,0:T(1,128)S(1)}, s32[1,1,32]{2,1,0:T(1,128)}, u32[]{:S(2)}) copy-start(s32[1,1,32]{2,1,0:T(1,128)} %param.9) | copy-start | bytes 388
  17.3 12.2 %copy-start.4 = (s32[1,1,32]{2,1,0:T(1,128)S(1)}, s32[1,1,32]{2,1,0:T(1,128)}, u32[]{:S(2)}) copy-start(s32[1,1,32]{2,1,0:T(1,128)} %param.10) | copy-start | bytes 388
  18.3 19.9 %all-to-all-start = ((bf16[4,4,128,256]{3,2,1,0:T(8,128)(2,1)}), bf16[4,4,128,256]{3,2,1,0:T(8,128)(2,1)S(1)}, u32[]{:S(2)}, u32[]{:S(2)}) async-start(bf16[4,4,128,256]{3,2,1,0:T(8,128)(2,1)} %shard_map.86), calls=%async_computation | async-start | bytes 2097152 | tf_op jit(solution)/shard_map/all_to_all | solution.py:123
  29.9 1.9 %copy-start.1 = (bf16[6144,256]{1,0:T(8,128)(2,1)S(1)}, bf16[6144,256]{1,0:T(8,128)(2,1)}, u32[]{:S(2)}) copy-start(bf16[6144,256]{1,0:T(8,128)(2,1)} %param.13) | copy-start | bytes 9437188
  31.8 6.4 %copy-start = (bf16[1,1,32,128,128]{4,3,2,1,0:T(8,128)(2,1)S(1)}, bf16[1,1,32,128,128]{4,3,2,1,0:T(8,128)(2,1)}, u32[]{:S(2)}) copy-start(bf16[1,1,32,128,128]{4,3,2,1,0:T(8,128)(2,1)} %param.8) | copy-start | bytes 3145732
  40.4 5.3 %collective-permute-start = (bf16[24,128,256]{2,1,0:T(8,128)(2,1)S(1)}, bf16[24,128,256]{2,1,0:T(8,128)(2,1)S(1)}, u32[]{:S(2)}, u32[]{:S(2)}) collective-permute-start(bf16[24,128,256]{2,1,0:T(8,128)(2,1)S(1)} %get-tuple-element.21), channel_id=1, source_target_pairs={{0,1},{1,0},{2,3},{3,2},{4,5},{5,4},{6,7},{7,6},{8,9},{9,8},{10,11... | collective-permute-start | bytes 4718600 | tf_op jit(solution)/shard_map/ppermute | solution.py:142
  46.1 14.8 %collective-permute-start.3 = (bf16[3,128,256]{2,1,0:T(8,128)(2,1)S(1)}, bf16[3,128,256]{2,1,0:T(8,128)(2,1)S(1)}, u32[]{:S(2)}, u32[]{:S(2)}) collective-permute-start(bf16[3,128,256]{2,1,0:T(8,128)(2,1)S(1)} %get-tuple-element.26), channel_id=1, source_target_pairs={{0,42},{1,7},{6,0},{7,13},{12,6},{13,19},{18,12},{19,25},{24,18},{... | collective-permute-start | bytes 589832 | tf_op jit(solution)/shard_map/ppermute | solution.py:150
  48.0 27.2 %collective-permute-start.1 = (bf16[3,128,256]{2,1,0:T(8,128)(2,1)S(1)}, bf16[3,128,256]{2,1,0:T(8,128)(2,1)S(1)}, u32[]{:S(2)}, u32[]{:S(2)}) collective-permute-start(bf16[3,128,256]{2,1,0:T(8,128)(2,1)S(1)} %get-tuple-element.23), channel_id=1, source_target_pairs={{0,6},{1,43},{6,12},{7,1},{12,18},{13,7},{18,24},{19,13},{24,30},{... | collective-permute-start | bytes 589832 | tf_op jit(solution)/shard_map/ppermute | solution.py:150
  51.9 23.3 %collective-permute-start.2 = (bf16[3,128,256]{2,1,0:T(8,128)(2,1)S(1)}, bf16[3,128,256]{2,1,0:T(8,128)(2,1)S(1)}, u32[]{:S(2)}, u32[]{:S(2)}) collective-permute-start(bf16[3,128,256]{2,1,0:T(8,128)(2,1)S(1)} %get-tuple-element.24), channel_id=1, source_target_pairs={{0,42},{1,7},{6,0},{7,13},{12,6},{13,19},{18,12},{19,25},{24,18},{... | collective-permute-start | bytes 589832 | tf_op jit(solution)/shard_map/ppermute | solution.py:150
  55.1 10.8 %collective-permute-start.5 = (bf16[3,128,256]{2,1,0:T(8,128)(2,1)S(1)}, bf16[3,128,256]{2,1,0:T(8,128)(2,1)S(1)}, u32[]{:S(2)}, u32[]{:S(2)}) collective-permute-start(bf16[3,128,256]{2,1,0:T(8,128)(2,1)S(1)} %get-tuple-element.28), channel_id=1, source_target_pairs={{0,12},{1,37},{6,18},{7,43},{12,24},{13,1},{18,30},{19,7},{24,36},... | collective-permute-start | bytes 589832 | tf_op jit(solution)/shard_map/ppermute | solution.py:150
  57.2 11.7 %collective-permute-start.6 = (bf16[3,128,256]{2,1,0:T(8,128)(2,1)S(1)}, bf16[3,128,256]{2,1,0:T(8,128)(2,1)S(1)}, u32[]{:S(2)}, u32[]{:S(2)}) collective-permute-start(bf16[3,128,256]{2,1,0:T(8,128)(2,1)S(1)} %get-tuple-element.29), channel_id=1, source_target_pairs={{0,6},{1,43},{6,12},{7,1},{12,18},{13,7},{18,24},{19,13},{24,30},{... | collective-permute-start | bytes 589832 | tf_op jit(solution)/shard_map/ppermute | solution.py:150
  60.9 48.1 %copy-start.2 = (bf16[256,256]{1,0:T(8,128)(2,1)S(1)}, bf16[256,256]{1,0:T(8,128)(2,1)}, u32[]{:S(2)}) copy-start(bf16[256,256]{1,0:T(8,128)(2,1)} %weight_ref.1) | copy-start | bytes 393220
  60.9 14.3 %collective-permute-start.4 = (bf16[3,128,256]{2,1,0:T(8,128)(2,1)S(1)}, bf16[3,128,256]{2,1,0:T(8,128)(2,1)S(1)}, u32[]{:S(2)}, u32[]{:S(2)}) collective-permute-start(bf16[3,128,256]{2,1,0:T(8,128)(2,1)S(1)} %add_convert_fusion.2), channel_id=1, source_target_pairs={{0,36},{1,13},{6,42},{7,19},{12,0},{13,25},{18,6},{19,31},{24,12},... | collective-permute-start | bytes 589832 | tf_op jit(solution)/shard_map/ppermute | solution.py:150
  69.0 11.3 %collective-permute-start.7 = (bf16[3,128,256]{2,1,0:T(8,128)(2,1)S(1)}, bf16[3,128,256]{2,1,0:T(8,128)(2,1)S(1)}, u32[]{:S(2)}, u32[]{:S(2)}) collective-permute-start(bf16[3,128,256]{2,1,0:T(8,128)(2,1)S(1)} %add_convert_fusion.1), channel_id=1, source_target_pairs={{0,12},{1,37},{6,18},{7,43},{12,24},{13,1},{18,30},{19,7},{24,36},... | collective-permute-start | bytes 589832 | tf_op jit(solution)/shard_map/ppermute | solution.py:150
  125.9 16.0 %collective-permute-start.8 = (bf16[12,128,256]{2,1,0:T(8,128)(2,1)S(1)}, bf16[12,128,256]{2,1,0:T(8,128)(2,1)S(1)}, u32[]{:S(2)}, u32[]{:S(2)}) collective-permute-start(bf16[12,128,256]{2,1,0:T(8,128)(2,1)S(1)} %all-gather.1.near_ref), channel_id=1, source_target_pairs={{0,6},{1,43},{6,0},{7,13},{12,18},{13,7},{18,12},{19,25},{24,30},{... | collective-permute-start | bytes 2359304 | tf_op jit(solution)/shard_map/ppermute | solution.py:159
  132.0 11.9 %collective-permute-start.9 = (bf16[12,128,256]{2,1,0:T(8,128)(2,1)S(1)}, bf16[12,128,256]{2,1,0:T(8,128)(2,1)S(1)}, u32[]{:S(2)}, u32[]{:S(2)}) collective-permute-start(bf16[12,128,256]{2,1,0:T(8,128)(2,1)S(1)} %all-gather.1.near_ref), channel_id=1, source_target_pairs={{0,1},{1,0},{2,3},{3,2},{4,5},{5,4},{6,7},{7,6},{8,9},{9,8},{10,11... | collective-permute-start | bytes 2359304 | tf_op jit(solution)/shard_map/ppermute | solution.py:142
  142.0 4.2 %collective-permute-start.10 = (bf16[12,128,256]{2,1,0:T(8,128)(2,1)S(1)}, bf16[12,128,256]{2,1,0:T(8,128)(2,1)S(1)}, u32[]{:S(2)}, u32[]{:S(2)}) collective-permute-start(bf16[12,128,256]{2,1,0:T(8,128)(2,1)S(1)} %collective-permute-done.8.far_ref), channel_id=1, source_target_pairs={{0,1},{1,0},{2,3},{3,2},{4,5},{5,4},{6,7},{7,6},{8,9},{9,8},{10,11... | collective-permute-start | bytes 2359304 | tf_op jit(solution)/shard_map/ppermute | solution.py:142

commit v5 on v4

--- a/solution.py
+++ b/solution.py
@@ -16,6 +16,8 @@
 BF = jnp.bfloat16
 F32 = jnp.float32
 UNROLL = 4
+SENT_STEPS = (3, 4, 5, 0, 1, 2, 6, 7)
+EARLY = 3
 SLOTS = 32
 
 
@@ -39,7 +41,7 @@
 
 
 def forward_kernel(
-    plan_ref, adj_ref, panels_ref, mine_ref, theirs_ref, acc_ref
+    plan_ref, adj_ref, panels_ref, early_mine_ref, mine_ref, early_theirs_ref, theirs_ref, acc_ref
 ):
     acc_ref[...] = jnp.zeros_like(acc_ref)
 
@@ -55,8 +57,11 @@
         return carry
 
     lax.fori_loop(0, plan_ref[2 * SLOTS] // UNROLL, step, 0)
-    theirs_ref[...] = acc_ref[HALF:].astype(BF)
-    mine_ref[...] = acc_ref[:HALF].astype(BF)
+    split = EARLY * ZH
+    early_theirs_ref[...] = acc_ref[HALF : HALF + split].astype(BF)
+    theirs_ref[...] = acc_ref[HALF + split :].astype(BF)
+    early_mine_ref[...] = acc_ref[:split].astype(BF)
+    mine_ref[...] = acc_ref[split:HALF].astype(BF)
 
 def chip_kernel(mine_ref, other_ref, *out_refs):
     for k, out_ref in enumerate(out_refs):
@@ -177,7 +182,10 @@
     row_ahead = (row_y - y) % Y
     foreign = (row_core != core).astype(jnp.int32)
     steps = jnp.where(row_core == 0, row_ahead, (Y - row_ahead) % Y)
-    sent_place = foreign * HALF + steps * ZH + row_zh
+    step_place = jnp.zeros_like(rows)
+    for place, k in enumerate(SENT_STEPS):
+        step_place = jnp.where(steps == k, place, step_place)
+    sent_place = foreign * HALF + step_place * ZH + row_zh
     gather_place = foreign * HALF + (row_ahead % 2) * QUARTER + row_y // YL * ZH + row_zh
 
     forward_plan = slot_plan(sent_place, cols, count)
@@ -205,22 +213,29 @@
     panels, own_grads, forward_plan, backward_plan = lax.optimization_barrier(
         (panels, own_grads, forward_plan, backward_plan)
     )
-    mine, theirs = pl.pallas_call(
+    early_mine, mine, early_theirs, theirs = pl.pallas_call(
         forward_kernel,
         out_shape=[
-            jax.ShapeDtypeStruct((HALF, TILE, F), BF),
-            jax.ShapeDtypeStruct((HALF, TILE, F), BF),
-        ],
+            jax.ShapeDtypeStruct((EARLY * ZH, TILE, F), BF),
+            jax.ShapeDtypeStruct(((Y - EARLY) * ZH, TILE, F), BF),
+        ]
+        * CORE,
         in_specs=[SMEM, VMEM, VMEM],
-        out_specs=[VMEM, VMEM],
+        out_specs=[VMEM] * 4,
         scratch_shapes=[pltpu.VMEM((CORE * HALF, TILE, F), F32)],
         compiler_params=params(18),
     )(forward_plan, adj, panels)
-    chip = pl.pallas_call(
-        chip_kernel,
-        out_shape=[jax.ShapeDtypeStruct((ZH, TILE, F), BF)] * Y,
-        compiler_params=params(8),
-    )(mine, swap_cores(theirs))
+    chip = {}
+    for steps_here, here_part, there_part in (
+        (SENT_STEPS[:EARLY], early_mine, early_theirs),
+        (SENT_STEPS[EARLY:], mine, theirs),
+    ):
+        sums = pl.pallas_call(
+            chip_kernel,
+            out_shape=[jax.ShapeDtypeStruct((ZH, TILE, F), BF)] * len(steps_here),
+            compiler_params=params(8),
+        )(here_part, swap_cores(there_part))
+        chip.update(zip(steps_here, sums))
     from_four = mirrored_shift(chip[4], 2)
     from_three = mirrored_shift(chip[3], 1)
     from_minus_three = mirrored_shift(chip[5], -1)

time: 184 us -> 182 us (0.989)
  starting transfers between devices: 48.1 us -> 42.8 us
  Pallas kernels: 6.62 us -> 8.65 us
    all_gather x1, blocking collectives: 16.1 us -> 22.9 us  [per_device(): near = lax.all_gather(here, 'yh', axis=0).reshape(QUARTER, TILE, F)]
    ppermute x7, starting transfers between devices: 25.8 us -> 21.6 us  [mirrored_shift(): return lax.ppermute(x, ('yh', 'yl', 'core'), pairs)]
    all_gather x1, blocking collectives: 28.5 us -> 24.2 us  [per_device(): parts = lax.all_gather(y_sum, 'zh', axis=0)]
    ppermute x1, starting transfers between devices: 6.06 us -> 2.68 us  [neighbour_exchange(): return lax.ppermute(x, ('yh', 'yl', 'core'), pairs)]
    ppermute x3 -> x4, starting transfers between devices: 5.75 us -> 8.16 us  [swap_cores(): return lax.ppermute(x, 'core', [(0, 1), (1, 0)])]
    ppermute x3 -> x4, waiting for transfers between devices: 5.62 us -> 3.85 us  [swap_cores(): return lax.ppermute(x, 'core', [(0, 1), (1, 0)])]
  transfers between devices with their start and end apart: 12 -> 13, of which waited for: 6 -> 6; matrix products, arithmetic and copies ran while one was open for 0% -> 0% of each run, Pallas kernels for 0% -> 0%
where the time goes in v5:
time: 182 us
  blocking collectives  96.2 us (53%)
  starting transfers between devices  42.8 us (24%)
  waiting for transfers between devices  28.8 us (16%)
  Pallas kernels  8.65 us (5%)
  local copies, waits for them, and re-layouts  2.29 us (1%)
    all_to_all x2, blocking collectives, exchange(): return lax.all_to_all(x, axis, 0, 0, tiled=True)  32.4 us
    all_gather x1, blocking collectives, per_device(): parts = lax.all_gather(y_sum, 'zh', axis=0)  24.2 us
    all_gather x1, blocking collectives, per_device(): near = lax.all_gather(here, 'yh', axis=0).reshape(QUARTER, TILE, F)  22.9 us
    ppermute x7, starting transfers between devices, mirrored_shift(): return lax.ppermute(x, ('yh', 'yl', 'core'), pairs)  21.6 us
    all_gather x1, blocking collectives, per_device(): panels = lax.all_gather(features[0], 'zl', axis=0)  16.7 us
    all_to_all x1, starting transfers between devices, exchange(): return lax.all_to_all(x, axis, 0, 0, tiled=True)  10.4 us
    ppermute x7, waiting for transfers between devices, mirrored_shift(): return lax.ppermute(x, ('yh', 'yl', 'core'), pairs)  9.63 us
    ppermute x1, waiting for transfers between devices, neighbour_exchange(): return lax.ppermute(x, ('yh', 'yl', 'core'), pairs)  9.25 us
  transfers between devices with their start and end apart: 13, of which 6 were waited for; matrix products, arithmetic and copies ran while one was open for 0% of the time, Pallas kernels for 0%

profile of v5, /device:TPU:2, one launch (start us, length us, event | category | flops | bytes accessed | tf_op | source)
XLA Modules:
  0.0 181.6 jit_solution(633932856012189164)
XLA Ops:
  0.6 16.7 %all_gather.15.x_ref = bf16[4,128,256]{2,1,0:T(8,128)(2,1)S(1)} all-gather(bf16[1,128,256]{2,1,0:T(8,128)(2,1)} %param.7), channel_id=1, replica_groups=mesh['x'=4,'zl'=4,'yh'=4,'yl'=2,'zh'=3,'core'=2] {'zl'}, dimensions={0}, use_global_device_ids=true | all-gather | bytes 327680 | tf_op jit(solution)/shard_map/all_gather | solution.py:194
  18.4 10.4 %all-to-all-start = ((bf16[4,4,128,256]{3,2,1,0:T(8,128)(2,1)}), bf16[4,4,128,256]{3,2,1,0:T(8,128)(2,1)S(1)}, u32[]{:S(2)}, u32[]{:S(2)}) async-start(bf16[4,4,128,256]{3,2,1,0:T(8,128)(2,1)} %shard_map.86), calls=%async_computation | async-start | bytes 2097152 | tf_op jit(solution)/shard_map/all_to_all | solution.py:128
  32.2 6.1 %all-to-all-done = bf16[4,4,128,256]{3,2,1,0:T(8,128)(2,1)S(1)} async-done(((bf16[4,4,128,256]{3,2,1,0:T(8,128)(2,1)}), bf16[4,4,128,256]{3,2,1,0:T(8,128)(2,1)S(1)}, u32[]{:S(2)}, u32[]{:S(2)}) %all-to-all-start) | async-done | bytes 1048608 | tf_op jit(solution)/shard_map/all_to_all | solution.py:128
  38.3 3.1 %shard_map.88 = (bf16[9,128,256]{2,1,0:T(8,128)(2,1)S(1)}, bf16[15,128,256]{2,1,0:T(8,128)(2,1)S(1)}, bf16[9,128,256]{2,1,0:T(8,128)(2,1)S(1)}, bf16[15,128,256]{2,1,0:T(8,128)(2,1)S(1)}) custom-call(s32[65]{0:T(128)S(1)} %get-tuple-element.20.plan_ref, bf16[32,128,128]{2,1,0:T(8,128)(2,1)S(1)} %bitcast.38, bf16[16,128,256]{2,1,0:T(8,128)(2,1)S(1)} %bitcast.37), custom_call_target="tpu_custom_call" | custom-call | tf_op jit(solution)/shard_map/pallas_call | solution.py:216
  41.4 1.9 %collective-permute-start = (bf16[15,128,256]{2,1,0:T(8,128)(2,1)S(1)}, bf16[15,128,256]{2,1,0:T(8,128)(2,1)S(1)}, u32[]{:S(2)}, u32[]{:S(2)}) collective-permute-start(bf16[15,128,256]{2,1,0:T(8,128)(2,1)S(1)} %get-tuple-element.23), channel_id=1, source_target_pairs={{0,1},{1,0},{2,3},{3,2},{4,5},{5,4},{6,7},{7,6},{8,9},{9,8},{10,11... | collective-permute-start | bytes 2949128 | tf_op jit(solution)/shard_map/ppermute | solution.py:147
  43.3 2.4 %collective-permute-start.3 = (bf16[9,128,256]{2,1,0:T(8,128)(2,1)S(1)}, bf16[9,128,256]{2,1,0:T(8,128)(2,1)S(1)}, u32[]{:S(2)}, u32[]{:S(2)}) collective-permute-start(bf16[9,128,256]{2,1,0:T(8,128)(2,1)S(1)} %get-tuple-element.29), channel_id=1, source_target_pairs={{0,1},{1,0},{2,3},{3,2},{4,5},{5,4},{6,7},{7,6},{8,9},{9,8},{10,11... | collective-permute-start | bytes 1769480 | tf_op jit(solution)/shard_map/ppermute | solution.py:147
  47.5 2.2 %collective-permute-start.4 = (bf16[3,128,256]{2,1,0:T(8,128)(2,1)S(1)}, bf16[3,128,256]{2,1,0:T(8,128)(2,1)S(1)}, u32[]{:S(2)}, u32[]{:S(2)}) collective-permute-start(bf16[3,128,256]{2,1,0:T(8,128)(2,1)S(1)} %get-tuple-element.30), channel_id=1, source_target_pairs={{0,42},{1,7},{6,0},{7,13},{12,6},{13,19},{18,12},{19,25},{24,18},{... | collective-permute-start | bytes 589832 | tf_op jit(solution)/shard_map/ppermute | solution.py:155
  49.7 1.9 %collective-permute-start.6 = (bf16[3,128,256]{2,1,0:T(8,128)(2,1)S(1)}, bf16[3,128,256]{2,1,0:T(8,128)(2,1)S(1)}, u32[]{:S(2)}, u32[]{:S(2)}) collective-permute-start(bf16[3,128,256]{2,1,0:T(8,128)(2,1)S(1)} %get-tuple-element.32), channel_id=1, source_target_pairs={{0,12},{1,37},{6,18},{7,43},{12,24},{13,1},{18,30},{19,7},{24,36},... | collective-permute-start | bytes 589832 | tf_op jit(solution)/shard_map/ppermute | solution.py:155
  51.6 3.6 %collective-permute-start.7 = (bf16[3,128,256]{2,1,0:T(8,128)(2,1)S(1)}, bf16[3,128,256]{2,1,0:T(8,128)(2,1)S(1)}, u32[]{:S(2)}, u32[]{:S(2)}) collective-permute-start(bf16[3,128,256]{2,1,0:T(8,128)(2,1)S(1)} %get-tuple-element.33), channel_id=1, source_target_pairs={{0,6},{1,43},{6,12},{7,1},{12,18},{13,7},{18,24},{19,13},{24,30},{... | collective-permute-start | bytes 589832 | tf_op jit(solution)/shard_map/ppermute | solution.py:155
  55.5 3.2 %collective-permute-start.1 = (bf16[3,128,256]{2,1,0:T(8,128)(2,1)S(1)}, bf16[3,128,256]{2,1,0:T(8,128)(2,1)S(1)}, u32[]{:S(2)}, u32[]{:S(2)}) collective-permute-start(bf16[3,128,256]{2,1,0:T(8,128)(2,1)S(1)} %get-tuple-element.25), channel_id=1, source_target_pairs={{0,6},{1,43},{6,12},{7,1},{12,18},{13,7},{18,24},{19,13},{24,30},{... | collective-permute-start | bytes 589832 | tf_op jit(solution)/shard_map/ppermute | solution.py:155
  58.7 3.8 %collective-permute-start.2 = (bf16[3,128,256]{2,1,0:T(8,128)(2,1)S(1)}, bf16[3,128,256]{2,1,0:T(8,128)(2,1)S(1)}, u32[]{:S(2)}, u32[]{:S(2)}) collective-permute-start(bf16[3,128,256]{2,1,0:T(8,128)(2,1)S(1)} %get-tuple-element.26), channel_id=1, source_target_pairs={{0,42},{1,7},{6,0},{7,13},{12,6},{13,19},{18,12},{19,25},{24,18},{... | collective-permute-start | bytes 589832 | tf_op jit(solution)/shard_map/ppermute | solution.py:155
  62.6 4.8 %collective-permute-start.5 = (bf16[3,128,256]{2,1,0:T(8,128)(2,1)S(1)}, bf16[3,128,256]{2,1,0:T(8,128)(2,1)S(1)}, u32[]{:S(2)}, u32[]{:S(2)}) collective-permute-start(bf16[3,128,256]{2,1,0:T(8,128)(2,1)S(1)} %add_convert_fusion.2), channel_id=1, source_target_pairs={{0,36},{1,13},{6,42},{7,19},{12,0},{13,25},{18,6},{19,31},{24,12},... | collective-permute-start | bytes 589832 | tf_op jit(solution)/shard_map/ppermute | solution.py:155
  67.6 1.9 %collective-permute-start.8 = (bf16[3,128,256]{2,1,0:T(8,128)(2,1)S(1)}, bf16[3,128,256]{2,1,0:T(8,128)(2,1)S(1)}, u32[]{:S(2)}, u32[]{:S(2)}) collective-permute-start(bf16[3,128,256]{2,1,0:T(8,128)(2,1)S(1)} %add_convert_fusion.1), channel_id=1, source_target_pairs={{0,12},{1,37},{6,18},{7,43},{12,24},{13,1},{18,30},{19,7},{24,36},... | collective-permute-start | bytes 589832 | tf_op jit(solution)/shard_map/ppermute | solution.py:155
  69.5 6.5 %collective-permute-done.5 = bf16[3,128,256]{2,1,0:T(8,128)(2,1)S(1)} collective-permute-done((bf16[3,128,256]{2,1,0:T(8,128)(2,1)S(1)}, bf16[3,128,256]{2,1,0:T(8,128)(2,1)S(1)}, u32[]{:S(2)}, u32[]{:S(2)}) %collective-permute-start.5) | collective-permute-done | bytes 196640 | tf_op jit(solution)/shard_map/ppermute | solution.py:155
  76.0 3.1 %collective-permute-done.8 = bf16[3,128,256]{2,1,0:T(8,128)(2,1)S(1)} collective-permute-done((bf16[3,128,256]{2,1,0:T(8,128)(2,1)S(1)}, bf16[3,128,256]{2,1,0:T(8,128)(2,1)S(1)}, u32[]{:S(2)}, u32[]{:S(2)}) %collective-permute-start.8) | collective-permute-done | bytes 196640 | tf_op jit(solution)/shard_map/ppermute | solution.py:155
  79.3 24.2 %all-gather = bf16[9,128,256]{2,1,0:T(8,128)(2,1)S(1)} all-gather(bf16[3,128,256]{2,1,0:T(8,128)(2,1)S(1)} %add_convert_fusion), channel_id=2, replica_groups=mesh['x'=4,'zl'=4,'yh'=4,'yl'=2,'zh'=3,'core'=2] {'zh'}, dimensions={0}, use_global_device_ids=true | all-gather | bytes 786432 | tf_op jit(solution)/shard_map/all_gather | solution.py:246
  104.4 22.9 %all-gather.1.near_ref = bf16[12,128,256]{2,1,0:T(8,128)(2,1)S(1)} all-gather(bf16[3,128,256]{2,1,0:T(8,128)(2,1)S(1)} %get-tuple-element.37), channel_id=3, replica_groups=mesh['x'=4,'zl'=4,'yh'=4,'yl'=2,'zh'=3,'core'=2] {'yh'}, dimensions={0}, use_global_device_ids=true | all-gather | bytes 983040 | tf_op jit(solution)/shard_map/all_gather | solution.py:260
  127.4 2.7 %collective-permute-start.9 = (bf16[12,128,256]{2,1,0:T(8,128)(2,1)S(1)}, bf16[12,128,256]{2,1,0:T(8,128)(2,1)S(1)}, u32[]{:S(2)}, u32[]{:S(2)}) collective-permute-start(bf16[12,128,256]{2,1,0:T(8,128)(2,1)S(1)} %all-gather.1.near_ref), channel_id=1, source_target_pairs={{0,6},{1,43},{6,0},{7,13},{12,18},{13,7},{18,12},{19,25},{24,30},{... | collective-permute-start | bytes 2359304 | tf_op jit(solution)/shard_map/ppermute | solution.py:164
  130.0 1.9 %collective-permute-start.10 = (bf16[12,128,256]{2,1,0:T(8,128)(2,1)S(1)}, bf16[12,128,256]{2,1,0:T(8,128)(2,1)S(1)}, u32[]{:S(2)}, u32[]{:S(2)}) collective-permute-start(bf16[12,128,256]{2,1,0:T(8,128)(2,1)S(1)} %all-gather.1.near_ref), channel_id=1, source_target_pairs={{0,1},{1,0},{2,3},{3,2},{4,5},{5,4},{6,7},{7,6},{8,9},{9,8},{10,11... | collective-permute-start | bytes 2359304 | tf_op jit(solution)/shard_map/ppermute | solution.py:147
  132.0 9.3 %collective-permute-done.9.far_ref = bf16[12,128,256]{2,1,0:T(8,128)(2,1)S(1)} collective-permute-done((bf16[12,128,256]{2,1,0:T(8,128)(2,1)S(1)}, bf16[12,128,256]{2,1,0:T(8,128)(2,1)S(1)}, u32[]{:S(2)}, u32[]{:S(2)}) %collective-permute-start.9) | collective-permute-done | bytes 786464 | tf_op jit(solution)/shard_map/ppermute | solution.py:164
  143.2 2.2 %collective-permute-done.11.other_far_ref = bf16[12,128,256]{2,1,0:T(8,128)(2,1)S(1)} collective-permute-done((bf16[12,128,256]{2,1,0:T(8,128)(2,1)S(1)}, bf16[12,128,256]{2,1,0:T(8,128)(2,1)S(1)}, u32[]{:S(2)}, u32[]{:S(2)}) %collective-permute-start.11) | collective-permute-done | bytes 786464 | tf_op jit(solution)/shard_map/ppermute | solution.py:147
  145.4 3.0 %shard_map.92 = bf16[16,128,256]{2,1,0:T(8,128)(2,1)S(1)} custom-call(s32[65]{0:T(128)S(1)} %get-tuple-element.36.plan_ref, bf16[32,128,128]{2,1,0:T(8,128)(2,1)S(1)} %bitcast.39, bf16[12,128,256]{2,1,0:T(8,128)(2,1)S(1)} %all-gather.1.near_ref, bf16[12,128,256]{2,1,0:T(8,128)(2,1)S(1)} %collective-permute-done.9.far_ref, ...), custom_call_target="tpu_custom_call" | custom-call | tf_op jit(solution)/shard_map/pallas_call | solution.py:263
  148.4 17.6 %all_to_all.15 = bf16[4,4,128,256]{3,2,1,0:T(8,128)(2,1)S(1)} all-to-all(bf16[4,4,128,256]{3,2,1,0:T(8,128)(2,1)S(1)} %bitcast.40), channel_id=1, replica_groups=mesh['x'=4,'zl'=4,'yh'=4,'yl'=2,'zh'=3,'core'=2] {'x'}, dimensions={0} | all-to-all | bytes 2097152 | tf_op jit(solution)/shard_map/all_to_all | solution.py:128
  166.2 14.8 %all_to_all.16 = bf16[4,128,256]{2,1,0:T(8,128)(2,1)S(1)} all-to-all(bf16[4,128,256]{2,1,0:T(8,128)(2,1)S(1)} %reduce_sum.24), channel_id=1, replica_groups=mesh['x'=4,'zl'=4,'yh'=4,'yl'=2,'zh'=3,'core'=2] {'zl'}, dimensions={0} | all-to-all | bytes 524288 | tf_op jit(solution)/shard_map/all_to_all | solution.py:128
  (37 shorter events, 9.7 us)
Async XLA Ops:
  0.6 28.8 %copy-start.3 = (s32[1,1,32]{2,1,0:T(1,128)S(1)}, s32[1,1,32]{2,1,0:T(1,128)}, u32[]{:S(2)}) copy-start(s32[1,1,32]{2,1,0:T(1,128)} %param.9) | copy-start | bytes 388
  0.6 28.9 %copy-start.4 = (s32[1,1,32]{2,1,0:T(1,128)S(1)}, s32[1,1,32]{2,1,0:T(1,128)}, u32[]{:S(2)}) copy-start(s32[1,1,32]{2,1,0:T(1,128)} %param.10) | copy-start | bytes 388
  17.3 20.9 %copy-start = (bf16[1,1,32,128,128]{4,3,2,1,0:T(8,128)(2,1)S(1)}, bf16[1,1,32,128,128]{4,3,2,1,0:T(8,128)(2,1)}, u32[]{:S(2)}) copy-start(bf16[1,1,32,128,128]{4,3,2,1,0:T(8,128)(2,1)} %param.8) | copy-start | bytes 3145732
  18.4 19.9 %all-to-all-start = ((bf16[4,4,128,256]{3,2,1,0:T(8,128)(2,1)}), bf16[4,4,128,256]{3,2,1,0:T(8,128)(2,1)S(1)}, u32[]{:S(2)}, u32[]{:S(2)}) async-start(bf16[4,4,128,256]{3,2,1,0:T(8,128)(2,1)} %shard_map.86), calls=%async_computation | async-start | bytes 2097152 | tf_op jit(solution)/shard_map/all_to_all | solution.py:128
  30.0 1.9 %copy-start.1 = (bf16[6144,256]{1,0:T(8,128)(2,1)S(1)}, bf16[6144,256]{1,0:T(8,128)(2,1)}, u32[]{:S(2)}) copy-start(bf16[6144,256]{1,0:T(8,128)(2,1)} %param.13) | copy-start | bytes 9437188
  41.4 13.9 %collective-permute-start = (bf16[15,128,256]{2,1,0:T(8,128)(2,1)S(1)}, bf16[15,128,256]{2,1,0:T(8,128)(2,1)S(1)}, u32[]{:S(2)}, u32[]{:S(2)}) collective-permute-start(bf16[15,128,256]{2,1,0:T(8,128)(2,1)S(1)} %get-tuple-element.23), channel_id=1, source_target_pairs={{0,1},{1,0},{2,3},{3,2},{4,5},{5,4},{6,7},{7,6},{8,9},{9,8},{10,11... | collective-permute-start | bytes 2949128 | tf_op jit(solution)/shard_map/ppermute | solution.py:147
  43.3 4.0 %collective-permute-start.3 = (bf16[9,128,256]{2,1,0:T(8,128)(2,1)S(1)}, bf16[9,128,256]{2,1,0:T(8,128)(2,1)S(1)}, u32[]{:S(2)}, u32[]{:S(2)}) collective-permute-start(bf16[9,128,256]{2,1,0:T(8,128)(2,1)S(1)} %get-tuple-element.29), channel_id=1, source_target_pairs={{0,1},{1,0},{2,3},{3,2},{4,5},{5,4},{6,7},{7,6},{8,9},{9,8},{10,11... | collective-permute-start | bytes 1769480 | tf_op jit(solution)/shard_map/ppermute | solution.py:147
  47.3 56.2 %copy-start.2 = (bf16[256,256]{1,0:T(8,128)(2,1)S(1)}, bf16[256,256]{1,0:T(8,128)(2,1)}, u32[]{:S(2)}) copy-start(bf16[256,256]{1,0:T(8,128)(2,1)} %weight_ref.1) | copy-start | bytes 393220
  47.5 15.1 %collective-permute-start.4 = (bf16[3,128,256]{2,1,0:T(8,128)(2,1)S(1)}, bf16[3,128,256]{2,1,0:T(8,128)(2,1)S(1)}, u32[]{:S(2)}, u32[]{:S(2)}) collective-permute-start(bf16[3,128,256]{2,1,0:T(8,128)(2,1)S(1)} %get-tuple-element.30), channel_id=1, source_target_pairs={{0,42},{1,7},{6,0},{7,13},{12,6},{13,19},{18,12},{19,25},{24,18},{... | collective-permute-start | bytes 589832 | tf_op jit(solution)/shard_map/ppermute | solution.py:155
  49.7 17.7 %collective-permute-start.6 = (bf16[3,128,256]{2,1,0:T(8,128)(2,1)S(1)}, bf16[3,128,256]{2,1,0:T(8,128)(2,1)S(1)}, u32[]{:S(2)}, u32[]{:S(2)}) collective-permute-start(bf16[3,128,256]{2,1,0:T(8,128)(2,1)S(1)} %get-tuple-element.32), channel_id=1, source_target_pairs={{0,12},{1,37},{6,18},{7,43},{12,24},{13,1},{18,30},{19,7},{24,36},... | collective-permute-start | bytes 589832 | tf_op jit(solution)/shard_map/ppermute | solution.py:155
  51.6 15.8 %collective-permute-start.7 = (bf16[3,128,256]{2,1,0:T(8,128)(2,1)S(1)}, bf16[3,128,256]{2,1,0:T(8,128)(2,1)S(1)}, u32[]{:S(2)}, u32[]{:S(2)}) collective-permute-start(bf16[3,128,256]{2,1,0:T(8,128)(2,1)S(1)} %get-tuple-element.33), channel_id=1, source_target_pairs={{0,6},{1,43},{6,12},{7,1},{12,18},{13,7},{18,24},{19,13},{24,30},{... | collective-permute-start | bytes 589832 | tf_op jit(solution)/shard_map/ppermute | solution.py:155
  55.5 14.0 %collective-permute-start.1 = (bf16[3,128,256]{2,1,0:T(8,128)(2,1)S(1)}, bf16[3,128,256]{2,1,0:T(8,128)(2,1)S(1)}, u32[]{:S(2)}, u32[]{:S(2)}) collective-permute-start(bf16[3,128,256]{2,1,0:T(8,128)(2,1)S(1)} %get-tuple-element.25), channel_id=1, source_target_pairs={{0,6},{1,43},{6,12},{7,1},{12,18},{13,7},{18,24},{19,13},{24,30},{... | collective-permute-start | bytes 589832 | tf_op jit(solution)/shard_map/ppermute | solution.py:155
  58.7 10.8 %collective-permute-start.2 = (bf16[3,128,256]{2,1,0:T(8,128)(2,1)S(1)}, bf16[3,128,256]{2,1,0:T(8,128)(2,1)S(1)}, u32[]{:S(2)}, u32[]{:S(2)}) collective-permute-start(bf16[3,128,256]{2,1,0:T(8,128)(2,1)S(1)} %get-tuple-element.26), channel_id=1, source_target_pairs={{0,42},{1,7},{6,0},{7,13},{12,6},{13,19},{18,12},{19,25},{24,18},{... | collective-permute-start | bytes 589832 | tf_op jit(solution)/shard_map/ppermute | solution.py:155
  62.6 13.4 %collective-permute-start.5 = (bf16[3,128,256]{2,1,0:T(8,128)(2,1)S(1)}, bf16[3,128,256]{2,1,0:T(8,128)(2,1)S(1)}, u32[]{:S(2)}, u32[]{:S(2)}) collective-permute-start(bf16[3,128,256]{2,1,0:T(8,128)(2,1)S(1)} %add_convert_fusion.2), channel_id=1, source_target_pairs={{0,36},{1,13},{6,42},{7,19},{12,0},{13,25},{18,6},{19,31},{24,12},... | collective-permute-start | bytes 589832 | tf_op jit(solution)/shard_map/ppermute | solution.py:155
  67.6 11.6 %collective-permute-start.8 = (bf16[3,128,256]{2,1,0:T(8,128)(2,1)S(1)}, bf16[3,128,256]{2,1,0:T(8,128)(2,1)S(1)}, u32[]{:S(2)}, u32[]{:S(2)}) collective-permute-start(bf16[3,128,256]{2,1,0:T(8,128)(2,1)S(1)} %add_convert_fusion.1), channel_id=1, source_target_pairs={{0,12},{1,37},{6,18},{7,43},{12,24},{13,1},{18,30},{19,7},{24,36},... | collective-permute-start | bytes 589832 | tf_op jit(solution)/shard_map/ppermute | solution.py:155
  127.4 13.9 %collective-permute-start.9 = (bf16[12,128,256]{2,1,0:T(8,128)(2,1)S(1)}, bf16[12,128,256]{2,1,0:T(8,128)(2,1)S(1)}, u32[]{:S(2)}, u32[]{:S(2)}) collective-permute-start(bf16[12,128,256]{2,1,0:T(8,128)(2,1)S(1)} %all-gather.1.near_ref), channel_id=1, source_target_pairs={{0,6},{1,43},{6,0},{7,13},{12,18},{13,7},{18,12},{19,25},{24,30},{... | collective-permute-start | bytes 2359304 | tf_op jit(solution)/shard_map/ppermute | solution.py:164
  130.0 13.1 %collective-permute-start.10 = (bf16[12,128,256]{2,1,0:T(8,128)(2,1)S(1)}, bf16[12,128,256]{2,1,0:T(8,128)(2,1)S(1)}, u32[]{:S(2)}, u32[]{:S(2)}) collective-permute-start(bf16[12,128,256]{2,1,0:T(8,128)(2,1)S(1)} %all-gather.1.near_ref), channel_id=1, source_target_pairs={{0,1},{1,0},{2,3},{3,2},{4,5},{5,4},{6,7},{7,6},{8,9},{9,8},{10,11... | collective-permute-start | bytes 2359304 | tf_op jit(solution)/shard_map/ppermute | solution.py:147
  141.2 4.2 %collective-permute-start.11 = (bf16[12,128,256]{2,1,0:T(8,128)(2,1)S(1)}, bf16[12,128,256]{2,1,0:T(8,128)(2,1)S(1)}, u32[]{:S(2)}, u32[]{:S(2)}) collective-permute-start(bf16[12,128,256]{2,1,0:T(8,128)(2,1)S(1)} %collective-permute-done.9.far_ref), channel_id=1, source_target_pairs={{0,1},{1,0},{2,3},{3,2},{4,5},{5,4},{6,7},{7,6},{8,9},{9,8},{10,11... | collective-permute-start | bytes 2359304 | tf_op jit(solution)/shard_map/ppermute | solution.py:147

commit v6 on v4

--- a/solution.py
+++ b/solution.py
@@ -58,10 +58,11 @@
     theirs_ref[...] = acc_ref[HALF:].astype(BF)
     mine_ref[...] = acc_ref[:HALF].astype(BF)
 
-def chip_kernel(mine_ref, other_ref, *out_refs):
-    for k, out_ref in enumerate(out_refs):
+def chip_kernel(mine_ref, other_ref, ahead_ref, *out_refs):
+    targets = [ahead_ref.at[:ZH], ahead_ref.at[ZH:], *out_refs]
+    for k, target in zip((1, 3, 0, 2, 4, 5, 6, 7), targets):
         at = slice(k * ZH, (k + 1) * ZH)
-        out_ref[...] = (mine_ref[at].astype(F32) + other_ref[at].astype(F32)).astype(BF)
+        target[...] = (mine_ref[at].astype(F32) + other_ref[at].astype(F32)).astype(BF)
 
 
 def backward_kernel(
@@ -216,15 +217,20 @@
         scratch_shapes=[pltpu.VMEM((CORE * HALF, TILE, F), F32)],
         compiler_params=params(18),
     )(forward_plan, adj, panels)
-    chip = pl.pallas_call(
+    to_next, *sums = pl.pallas_call(
         chip_kernel,
-        out_shape=[jax.ShapeDtypeStruct((ZH, TILE, F), BF)] * Y,
+        out_shape=[
+            jax.ShapeDtypeStruct((2 * ZH, TILE, F), BF),
+            *[jax.ShapeDtypeStruct((ZH, TILE, F), BF)] * (Y - 2),
+        ],
         compiler_params=params(8),
     )(mine, swap_cores(theirs))
+    chip = dict(zip((0, 2, 4, 5, 6, 7), sums))
     from_four = mirrored_shift(chip[4], 2)
-    from_three = mirrored_shift(chip[3], 1)
+    from_behind = mirrored_shift(to_next, 1)
+    from_one, from_three = from_behind[:ZH], from_behind[ZH:]
     from_minus_three = mirrored_shift(chip[5], -1)
-    ones = [mirrored_shift(chip[1], 1), mirrored_shift(chip[7], -1)]
+    ones = [from_one, mirrored_shift(chip[7], -1)]
     minus_two = mirrored_shift(add_up(chip[6], from_minus_three), -2)
     plus_two = mirrored_shift(add_up(chip[2], from_four, from_three), 2)
     y_sum = add_up(chip[0], *ones, minus_two, plus_two)

time: 184 us -> 180 us (0.978)
  starting transfers between devices: 48.1 us -> 37.3 us
  waiting for transfers between devices: 27.9 us -> 36.3 us
  Pallas kernels: 6.62 us -> 8.64 us
  blocking collectives: 94.8 us -> 92.9 us
    ppermute x7 -> x6, starting transfers between devices: 25.8 us -> 19.2 us  [mirrored_shift(): return lax.ppermute(x, ('yh', 'yl', 'core'), pairs)]
    ppermute x7 -> x6, waiting for transfers between devices: 8.17 us -> 14.6 us  [mirrored_shift(): return lax.ppermute(x, ('yh', 'yl', 'core'), pairs)]
    all_gather x1, blocking collectives: 16.1 us -> 20.3 us  [per_device(): near = lax.all_gather(here, 'yh', axis=0).reshape(QUARTER, TILE, F)]
    ppermute x1, starting transfers between devices: 6.06 us -> 1.91 us  [neighbour_exchange(): return lax.ppermute(x, ('yh', 'yl', 'core'), pairs)]
    all_gather x1, blocking collectives: 28.5 us -> 24.7 us  [per_device(): parts = lax.all_gather(y_sum, 'zh', axis=0)]
    all_to_all x2, blocking collectives: 33.6 us -> 31.3 us  [exchange(): return lax.all_to_all(x, axis, 0, 0, tiled=True)]
    ppermute x1, waiting for transfers between devices: 8.03 us -> 10 us  [neighbour_exchange(): return lax.ppermute(x, ('yh', 'yl', 'core'), pairs)]
  transfers between devices with their start and end apart: 12 -> 11, of which waited for: 6 -> 6; matrix products, arithmetic and copies ran while one was open for 0% -> 0% of each run, Pallas kernels for 0% -> 0%
where the time goes in v6:
time: 180 us
  blocking collectives  92.9 us (52%)
  starting transfers between devices  37.3 us (21%)
  waiting for transfers between devices  36.3 us (20%)
  Pallas kernels  8.64 us (5%)
  local copies, waits for them, and re-layouts  2.29 us (1%)
    all_to_all x2, blocking collectives, exchange(): return lax.all_to_all(x, axis, 0, 0, tiled=True)  31.3 us
    all_gather x1, blocking collectives, per_device(): parts = lax.all_gather(y_sum, 'zh', axis=0)  24.7 us
    all_gather x1, blocking collectives, per_device(): near = lax.all_gather(here, 'yh', axis=0).reshape(QUARTER, TILE, F)  20.3 us
    ppermute x6, starting transfers between devices, mirrored_shift(): return lax.ppermute(x, ('yh', 'yl', 'core'), pairs)  19.2 us
    all_gather x1, blocking collectives, per_device(): panels = lax.all_gather(features[0], 'zl', axis=0)  16.7 us
    ppermute x6, waiting for transfers between devices, mirrored_shift(): return lax.ppermute(x, ('yh', 'yl', 'core'), pairs)  14.6 us
    all_to_all x1, starting transfers between devices, exchange(): return lax.all_to_all(x, axis, 0, 0, tiled=True)  10.4 us
    ppermute x1, waiting for transfers between devices, neighbour_exchange(): return lax.ppermute(x, ('yh', 'yl', 'core'), pairs)  10 us
  transfers between devices with their start and end apart: 11, of which 6 were waited for; matrix products, arithmetic and copies ran while one was open for 0% of the time, Pallas kernels for 0%

profile of v6, /device:TPU:2, one launch (start us, length us, event | category | flops | bytes accessed | tf_op | source)
XLA Modules:
  0.0 180.2 jit_solution(1946977831106707085)
XLA Ops:
  0.6 16.7 %all_gather.15.x_ref = bf16[4,128,256]{2,1,0:T(8,128)(2,1)S(1)} all-gather(bf16[1,128,256]{2,1,0:T(8,128)(2,1)} %param.7), channel_id=1, replica_groups=mesh['x'=4,'zl'=4,'yh'=4,'yl'=2,'zh'=3,'core'=2] {'zl'}, dimensions={0}, use_global_device_ids=true | all-gather | bytes 327680 | tf_op jit(solution)/shard_map/all_gather | solution.py:187
  18.3 10.4 %all-to-all-start = ((bf16[4,4,128,256]{3,2,1,0:T(8,128)(2,1)}), bf16[4,4,128,256]{3,2,1,0:T(8,128)(2,1)S(1)}, u32[]{:S(2)}, u32[]{:S(2)}) async-start(bf16[4,4,128,256]{3,2,1,0:T(8,128)(2,1)} %shard_map.86), calls=%async_computation | async-start | bytes 2097152 | tf_op jit(solution)/shard_map/all_to_all | solution.py:124
  32.2 6.1 %all-to-all-done = bf16[4,4,128,256]{3,2,1,0:T(8,128)(2,1)S(1)} async-done(((bf16[4,4,128,256]{3,2,1,0:T(8,128)(2,1)}), bf16[4,4,128,256]{3,2,1,0:T(8,128)(2,1)S(1)}, u32[]{:S(2)}, u32[]{:S(2)}) %all-to-all-start) | async-done | bytes 1048608 | tf_op jit(solution)/shard_map/all_to_all | solution.py:124
  38.2 3.1 %shard_map.88 = (bf16[24,128,256]{2,1,0:T(8,128)(2,1)S(1)}, bf16[24,128,256]{2,1,0:T(8,128)(2,1)S(1)}) custom-call(s32[65]{0:T(128)S(1)} %get-tuple-element.17.plan_ref, bf16[32,128,128]{2,1,0:T(8,128)(2,1)S(1)} %bitcast.38, bf16[16,128,256]{2,1,0:T(8,128)(2,1)S(1)} %bitcast.37), custom_call_target="tpu_custom_call" | custom-call | tf_op jit(solution)/shard_map/pallas_call | solution.py:209
  41.3 1.9 %collective-permute-start = (bf16[24,128,256]{2,1,0:T(8,128)(2,1)S(1)}, bf16[24,128,256]{2,1,0:T(8,128)(2,1)S(1)}, u32[]{:S(2)}, u32[]{:S(2)}) collective-permute-start(bf16[24,128,256]{2,1,0:T(8,128)(2,1)S(1)} %get-tuple-element.20), channel_id=1, source_target_pairs={{0,1},{1,0},{2,3},{3,2},{4,5},{5,4},{6,7},{7,6},{8,9},{9,8},{10,11... | collective-permute-start | bytes 4718600 | tf_op jit(solution)/shard_map/ppermute | solution.py:143
  43.3 3.4 %collective-permute-done.other_ref = bf16[24,128,256]{2,1,0:T(8,128)(2,1)S(1)} collective-permute-done((bf16[24,128,256]{2,1,0:T(8,128)(2,1)S(1)}, bf16[24,128,256]{2,1,0:T(8,128)(2,1)S(1)}, u32[]{:S(2)}, u32[]{:S(2)}) %collective-permute-start) | collective-permute-done | bytes 1572896 | tf_op jit(solution)/shard_map/ppermute | solution.py:143
  47.0 2.3 %collective-permute-start.3 = (bf16[3,128,256]{2,1,0:T(8,128)(2,1)S(1)}, bf16[3,128,256]{2,1,0:T(8,128)(2,1)S(1)}, u32[]{:S(2)}, u32[]{:S(2)}) collective-permute-start(bf16[3,128,256]{2,1,0:T(8,128)(2,1)S(1)} %get-tuple-element.25), channel_id=1, source_target_pairs={{0,42},{1,7},{6,0},{7,13},{12,6},{13,19},{18,12},{19,25},{24,18},{... | collective-permute-start | bytes 589832 | tf_op jit(solution)/shard_map/ppermute | solution.py:151
  49.3 3.6 %collective-permute-start.1 = (bf16[6,128,256]{2,1,0:T(8,128)(2,1)S(1)}, bf16[6,128,256]{2,1,0:T(8,128)(2,1)S(1)}, u32[]{:S(2)}, u32[]{:S(2)}) collective-permute-start(bf16[6,128,256]{2,1,0:T(8,128)(2,1)S(1)} %get-tuple-element.22), channel_id=1, source_target_pairs={{0,6},{1,43},{6,12},{7,1},{12,18},{13,7},{18,24},{19,13},{24,30},{... | collective-permute-start | bytes 1179656 | tf_op jit(solution)/shard_map/ppermute | solution.py:151
  52.9 3.5 %collective-permute-start.2 = (bf16[3,128,256]{2,1,0:T(8,128)(2,1)S(1)}, bf16[3,128,256]{2,1,0:T(8,128)(2,1)S(1)}, u32[]{:S(2)}, u32[]{:S(2)}) collective-permute-start(bf16[3,128,256]{2,1,0:T(8,128)(2,1)S(1)} %get-tuple-element.23), channel_id=1, source_target_pairs={{0,42},{1,7},{6,0},{7,13},{12,6},{13,19},{18,12},{19,25},{24,18},{... | collective-permute-start | bytes 589832 | tf_op jit(solution)/shard_map/ppermute | solution.py:151
  56.3 1.9 %collective-permute-start.5 = (bf16[3,128,256]{2,1,0:T(8,128)(2,1)S(1)}, bf16[3,128,256]{2,1,0:T(8,128)(2,1)S(1)}, u32[]{:S(2)}, u32[]{:S(2)}) collective-permute-start(bf16[3,128,256]{2,1,0:T(8,128)(2,1)S(1)} %get-tuple-element.27), channel_id=1, source_target_pairs={{0,12},{1,37},{6,18},{7,43},{12,24},{13,1},{18,30},{19,7},{24,36},... | collective-permute-start | bytes 589832 | tf_op jit(solution)/shard_map/ppermute | solution.py:151
  58.3 6.0 %collective-permute-start.4 = (bf16[3,128,256]{2,1,0:T(8,128)(2,1)S(1)}, bf16[3,128,256]{2,1,0:T(8,128)(2,1)S(1)}, u32[]{:S(2)}, u32[]{:S(2)}) collective-permute-start(bf16[3,128,256]{2,1,0:T(8,128)(2,1)S(1)} %add_convert_fusion.2), channel_id=1, source_target_pairs={{0,36},{1,13},{6,42},{7,19},{12,0},{13,25},{18,6},{19,31},{24,12},... | collective-permute-start | bytes 589832 | tf_op jit(solution)/shard_map/ppermute | solution.py:151
  64.4 6.9 %collective-permute-done.5 = bf16[3,128,256]{2,1,0:T(8,128)(2,1)S(1)} collective-permute-done((bf16[3,128,256]{2,1,0:T(8,128)(2,1)S(1)}, bf16[3,128,256]{2,1,0:T(8,128)(2,1)S(1)}, u32[]{:S(2)}, u32[]{:S(2)}) %collective-permute-start.5) | collective-permute-done | bytes 196640 | tf_op jit(solution)/shard_map/ppermute | solution.py:151
  71.3 1.9 %collective-permute-start.6 = (bf16[3,128,256]{2,1,0:T(8,128)(2,1)S(1)}, bf16[3,128,256]{2,1,0:T(8,128)(2,1)S(1)}, u32[]{:S(2)}, u32[]{:S(2)}) collective-permute-start(bf16[3,128,256]{2,1,0:T(8,128)(2,1)S(1)} %add_convert_fusion.1), channel_id=1, source_target_pairs={{0,12},{1,37},{6,18},{7,43},{12,24},{13,1},{18,30},{19,7},{24,36},... | collective-permute-start | bytes 589832 | tf_op jit(solution)/shard_map/ppermute | solution.py:151
  73.3 7.7 %collective-permute-done.6 = bf16[3,128,256]{2,1,0:T(8,128)(2,1)S(1)} collective-permute-done((bf16[3,128,256]{2,1,0:T(8,128)(2,1)S(1)}, bf16[3,128,256]{2,1,0:T(8,128)(2,1)S(1)}, u32[]{:S(2)}, u32[]{:S(2)}) %collective-permute-start.6) | collective-permute-done | bytes 196640 | tf_op jit(solution)/shard_map/ppermute | solution.py:151
  81.1 24.7 %all-gather = bf16[9,128,256]{2,1,0:T(8,128)(2,1)S(1)} all-gather(bf16[3,128,256]{2,1,0:T(8,128)(2,1)S(1)} %add_convert_fusion), channel_id=2, replica_groups=mesh['x'=4,'zl'=4,'yh'=4,'yl'=2,'zh'=3,'core'=2] {'zh'}, dimensions={0}, use_global_device_ids=true | all-gather | bytes 786432 | tf_op jit(solution)/shard_map/all_gather | solution.py:237
  106.7 20.3 %all-gather.1.near_ref = bf16[12,128,256]{2,1,0:T(8,128)(2,1)S(1)} all-gather(bf16[3,128,256]{2,1,0:T(8,128)(2,1)S(1)} %get-tuple-element.31), channel_id=3, replica_groups=mesh['x'=4,'zl'=4,'yh'=4,'yl'=2,'zh'=3,'core'=2] {'yh'}, dimensions={0}, use_global_device_ids=true | all-gather | bytes 983040 | tf_op jit(solution)/shard_map/all_gather | solution.py:251
  127.1 1.9 %collective-permute-start.7 = (bf16[12,128,256]{2,1,0:T(8,128)(2,1)S(1)}, bf16[12,128,256]{2,1,0:T(8,128)(2,1)S(1)}, u32[]{:S(2)}, u32[]{:S(2)}) collective-permute-start(bf16[12,128,256]{2,1,0:T(8,128)(2,1)S(1)} %all-gather.1.near_ref), channel_id=1, source_target_pairs={{0,6},{1,43},{6,0},{7,13},{12,18},{13,7},{18,12},{19,25},{24,30},{... | collective-permute-start | bytes 2359304 | tf_op jit(solution)/shard_map/ppermute | solution.py:160
  129.0 1.9 %collective-permute-start.8 = (bf16[12,128,256]{2,1,0:T(8,128)(2,1)S(1)}, bf16[12,128,256]{2,1,0:T(8,128)(2,1)S(1)}, u32[]{:S(2)}, u32[]{:S(2)}) collective-permute-start(bf16[12,128,256]{2,1,0:T(8,128)(2,1)S(1)} %all-gather.1.near_ref), channel_id=1, source_target_pairs={{0,1},{1,0},{2,3},{3,2},{4,5},{5,4},{6,7},{7,6},{8,9},{9,8},{10,11... | collective-permute-start | bytes 2359304 | tf_op jit(solution)/shard_map/ppermute | solution.py:143
  130.9 10.0 %collective-permute-done.7.far_ref = bf16[12,128,256]{2,1,0:T(8,128)(2,1)S(1)} collective-permute-done((bf16[12,128,256]{2,1,0:T(8,128)(2,1)S(1)}, bf16[12,128,256]{2,1,0:T(8,128)(2,1)S(1)}, u32[]{:S(2)}, u32[]{:S(2)}) %collective-permute-start.7) | collective-permute-done | bytes 786464 | tf_op jit(solution)/shard_map/ppermute | solution.py:160
  140.9 1.9 %collective-permute-start.9 = (bf16[12,128,256]{2,1,0:T(8,128)(2,1)S(1)}, bf16[12,128,256]{2,1,0:T(8,128)(2,1)S(1)}, u32[]{:S(2)}, u32[]{:S(2)}) collective-permute-start(bf16[12,128,256]{2,1,0:T(8,128)(2,1)S(1)} %collective-permute-done.7.far_ref), channel_id=1, source_target_pairs={{0,1},{1,0},{2,3},{3,2},{4,5},{5,4},{6,7},{7,6},{8,9},{9,8},{10,11... | collective-permute-start | bytes 2359304 | tf_op jit(solution)/shard_map/ppermute | solution.py:143
  142.9 2.2 %collective-permute-done.9.other_far_ref = bf16[12,128,256]{2,1,0:T(8,128)(2,1)S(1)} collective-permute-done((bf16[12,128,256]{2,1,0:T(8,128)(2,1)S(1)}, bf16[12,128,256]{2,1,0:T(8,128)(2,1)S(1)}, u32[]{:S(2)}, u32[]{:S(2)}) %collective-permute-start.9) | collective-permute-done | bytes 786464 | tf_op jit(solution)/shard_map/ppermute | solution.py:143
  145.1 3.0 %shard_map.91 = bf16[16,128,256]{2,1,0:T(8,128)(2,1)S(1)} custom-call(s32[65]{0:T(128)S(1)} %get-tuple-element.30.plan_ref, bf16[32,128,128]{2,1,0:T(8,128)(2,1)S(1)} %bitcast.39, bf16[12,128,256]{2,1,0:T(8,128)(2,1)S(1)} %all-gather.1.near_ref, bf16[12,128,256]{2,1,0:T(8,128)(2,1)S(1)} %collective-permute-done.7.far_ref, ...), custom_call_target="tpu_custom_call" | custom-call | tf_op jit(solution)/shard_map/pallas_call | solution.py:254
  148.1 17.5 %all_to_all.15 = bf16[4,4,128,256]{3,2,1,0:T(8,128)(2,1)S(1)} all-to-all(bf16[4,4,128,256]{3,2,1,0:T(8,128)(2,1)S(1)} %bitcast.40), channel_id=1, replica_groups=mesh['x'=4,'zl'=4,'yh'=4,'yl'=2,'zh'=3,'core'=2] {'x'}, dimensions={0} | all-to-all | bytes 2097152 | tf_op jit(solution)/shard_map/all_to_all | solution.py:124
  165.8 13.7 %all_to_all.16 = bf16[4,128,256]{2,1,0:T(8,128)(2,1)S(1)} all-to-all(bf16[4,128,256]{2,1,0:T(8,128)(2,1)S(1)} %reduce_sum.24), channel_id=1, replica_groups=mesh['x'=4,'zl'=4,'yh'=4,'yl'=2,'zh'=3,'core'=2] {'zl'}, dimensions={0} | all-to-all | bytes 524288 | tf_op jit(solution)/shard_map/all_to_all | solution.py:124
  (32 shorter events, 6.2 us)
Async XLA Ops:
  17.3 12.2 %copy-start.3 = (s32[1,1,32]{2,1,0:T(1,128)S(1)}, s32[1,1,32]{2,1,0:T(1,128)}, u32[]{:S(2)}) copy-start(s32[1,1,32]{2,1,0:T(1,128)} %param.9) | copy-start | bytes 388
  17.3 12.2 %copy-start.4 = (s32[1,1,32]{2,1,0:T(1,128)S(1)}, s32[1,1,32]{2,1,0:T(1,128)}, u32[]{:S(2)}) copy-start(s32[1,1,32]{2,1,0:T(1,128)} %param.10) | copy-start | bytes 388
  18.3 19.9 %all-to-all-start = ((bf16[4,4,128,256]{3,2,1,0:T(8,128)(2,1)}), bf16[4,4,128,256]{3,2,1,0:T(8,128)(2,1)S(1)}, u32[]{:S(2)}, u32[]{:S(2)}) async-start(bf16[4,4,128,256]{3,2,1,0:T(8,128)(2,1)} %shard_map.86), calls=%async_computation | async-start | bytes 2097152 | tf_op jit(solution)/shard_map/all_to_all | solution.py:124
  29.9 1.9 %copy-start.1 = (bf16[6144,256]{1,0:T(8,128)(2,1)S(1)}, bf16[6144,256]{1,0:T(8,128)(2,1)}, u32[]{:S(2)}) copy-start(bf16[6144,256]{1,0:T(8,128)(2,1)} %param.13) | copy-start | bytes 9437188
  31.8 6.4 %copy-start = (bf16[1,1,32,128,128]{4,3,2,1,0:T(8,128)(2,1)S(1)}, bf16[1,1,32,128,128]{4,3,2,1,0:T(8,128)(2,1)}, u32[]{:S(2)}) copy-start(bf16[1,1,32,128,128]{4,3,2,1,0:T(8,128)(2,1)} %param.8) | copy-start | bytes 3145732
  41.3 5.3 %collective-permute-start = (bf16[24,128,256]{2,1,0:T(8,128)(2,1)S(1)}, bf16[24,128,256]{2,1,0:T(8,128)(2,1)S(1)}, u32[]{:S(2)}, u32[]{:S(2)}) collective-permute-start(bf16[24,128,256]{2,1,0:T(8,128)(2,1)S(1)} %get-tuple-element.20), channel_id=1, source_target_pairs={{0,1},{1,0},{2,3},{3,2},{4,5},{5,4},{6,7},{7,6},{8,9},{9,8},{10,11... | collective-permute-start | bytes 4718600 | tf_op jit(solution)/shard_map/ppermute | solution.py:143
  47.0 11.3 %collective-permute-start.3 = (bf16[3,128,256]{2,1,0:T(8,128)(2,1)S(1)}, bf16[3,128,256]{2,1,0:T(8,128)(2,1)S(1)}, u32[]{:S(2)}, u32[]{:S(2)}) collective-permute-start(bf16[3,128,256]{2,1,0:T(8,128)(2,1)S(1)} %get-tuple-element.25), channel_id=1, source_target_pairs={{0,42},{1,7},{6,0},{7,13},{12,6},{13,19},{18,12},{19,25},{24,18},{... | collective-permute-start | bytes 589832 | tf_op jit(solution)/shard_map/ppermute | solution.py:151
  49.3 22.0 %collective-permute-start.1 = (bf16[6,128,256]{2,1,0:T(8,128)(2,1)S(1)}, bf16[6,128,256]{2,1,0:T(8,128)(2,1)S(1)}, u32[]{:S(2)}, u32[]{:S(2)}) collective-permute-start(bf16[6,128,256]{2,1,0:T(8,128)(2,1)S(1)} %get-tuple-element.22), channel_id=1, source_target_pairs={{0,6},{1,43},{6,12},{7,1},{12,18},{13,7},{18,24},{19,13},{24,30},{... | collective-permute-start | bytes 1179656 | tf_op jit(solution)/shard_map/ppermute | solution.py:151
  52.9 20.4 %collective-permute-start.2 = (bf16[3,128,256]{2,1,0:T(8,128)(2,1)S(1)}, bf16[3,128,256]{2,1,0:T(8,128)(2,1)S(1)}, u32[]{:S(2)}, u32[]{:S(2)}) collective-permute-start(bf16[3,128,256]{2,1,0:T(8,128)(2,1)S(1)} %get-tuple-element.23), channel_id=1, source_target_pairs={{0,42},{1,7},{6,0},{7,13},{12,6},{13,19},{18,12},{19,25},{24,18},{... | collective-permute-start | bytes 589832 | tf_op jit(solution)/shard_map/ppermute | solution.py:151
  56.3 14.9 %collective-permute-start.5 = (bf16[3,128,256]{2,1,0:T(8,128)(2,1)S(1)}, bf16[3,128,256]{2,1,0:T(8,128)(2,1)S(1)}, u32[]{:S(2)}, u32[]{:S(2)}) collective-permute-start(bf16[3,128,256]{2,1,0:T(8,128)(2,1)S(1)} %get-tuple-element.27), channel_id=1, source_target_pairs={{0,12},{1,37},{6,18},{7,43},{12,24},{13,1},{18,30},{19,7},{24,36},... | collective-permute-start | bytes 589832 | tf_op jit(solution)/shard_map/ppermute | solution.py:151
  58.3 47.6 %copy-start.2 = (bf16[256,256]{1,0:T(8,128)(2,1)S(1)}, bf16[256,256]{1,0:T(8,128)(2,1)}, u32[]{:S(2)}) copy-start(bf16[256,256]{1,0:T(8,128)(2,1)} %weight_ref.1) | copy-start | bytes 393220
  58.3 14.9 %collective-permute-start.4 = (bf16[3,128,256]{2,1,0:T(8,128)(2,1)S(1)}, bf16[3,128,256]{2,1,0:T(8,128)(2,1)S(1)}, u32[]{:S(2)}, u32[]{:S(2)}) collective-permute-start(bf16[3,128,256]{2,1,0:T(8,128)(2,1)S(1)} %add_convert_fusion.2), channel_id=1, source_target_pairs={{0,36},{1,13},{6,42},{7,19},{12,0},{13,25},{18,6},{19,31},{24,12},... | collective-permute-start | bytes 589832 | tf_op jit(solution)/shard_map/ppermute | solution.py:151
  71.3 9.7 %collective-permute-start.6 = (bf16[3,128,256]{2,1,0:T(8,128)(2,1)S(1)}, bf16[3,128,256]{2,1,0:T(8,128)(2,1)S(1)}, u32[]{:S(2)}, u32[]{:S(2)}) collective-permute-start(bf16[3,128,256]{2,1,0:T(8,128)(2,1)S(1)} %add_convert_fusion.1), channel_id=1, source_target_pairs={{0,12},{1,37},{6,18},{7,43},{12,24},{13,1},{18,30},{19,7},{24,36},... | collective-permute-start | bytes 589832 | tf_op jit(solution)/shard_map/ppermute | solution.py:151
  127.1 13.9 %collective-permute-start.7 = (bf16[12,128,256]{2,1,0:T(8,128)(2,1)S(1)}, bf16[12,128,256]{2,1,0:T(8,128)(2,1)S(1)}, u32[]{:S(2)}, u32[]{:S(2)}) collective-permute-start(bf16[12,128,256]{2,1,0:T(8,128)(2,1)S(1)} %all-gather.1.near_ref), channel_id=1, source_target_pairs={{0,6},{1,43},{6,0},{7,13},{12,18},{13,7},{18,12},{19,25},{24,30},{... | collective-permute-start | bytes 2359304 | tf_op jit(solution)/shard_map/ppermute | solution.py:160
  129.0 13.9 %collective-permute-start.8 = (bf16[12,128,256]{2,1,0:T(8,128)(2,1)S(1)}, bf16[12,128,256]{2,1,0:T(8,128)(2,1)S(1)}, u32[]{:S(2)}, u32[]{:S(2)}) collective-permute-start(bf16[12,128,256]{2,1,0:T(8,128)(2,1)S(1)} %all-gather.1.near_ref), channel_id=1, source_target_pairs={{0,1},{1,0},{2,3},{3,2},{4,5},{5,4},{6,7},{7,6},{8,9},{9,8},{10,11... | collective-permute-start | bytes 2359304 | tf_op jit(solution)/shard_map/ppermute | solution.py:143
  140.9 4.2 %collective-permute-start.9 = (bf16[12,128,256]{2,1,0:T(8,128)(2,1)S(1)}, bf16[12,128,256]{2,1,0:T(8,128)(2,1)S(1)}, u32[]{:S(2)}, u32[]{:S(2)}) collective-permute-start(bf16[12,128,256]{2,1,0:T(8,128)(2,1)S(1)} %collective-permute-done.7.far_ref), channel_id=1, source_target_pairs={{0,1},{1,0},{2,3},{3,2},{4,5},{5,4},{6,7},{7,6},{8,9},{9,8},{10,11... | collective-permute-start | bytes 2359304 | tf_op jit(solution)/shard_map/ppermute | solution.py:143
